TPU v7x, 512 devices: a whole 4x4x16 slice. The times are simulated.
512 devices in a mesh: dp: 32 (over x_hi, z), test: 16 (over y, x_lo, core).
Axes of the slice: x: 4 (x_hi: 2, x_lo: 2; x = x_hi * 2 + x_lo), y: 4, z: 16, core: 2. Of those that a mesh axis runs over, the one named last changes fastest.
Arguments:
- tokens: bfloat16 [8192, 4096], P('dp', 'test'), may hold values from -6 to 6
- upstream: bfloat16 [8192, 4096], P('dp', 'test'), may hold values from -6 to 6
- rewards: float32 [32, 2], P('dp'), may hold values from -8 to 8
- lengths: int32 [32, 2], P('dp'), may hold values from 1 to 128, as said below
- gate_weight: bfloat16 [4096, 8192], P('dp', 'test'), may hold values from -0.09375 to 0.09375
- up_weight: bfloat16 [4096, 8192], P('dp', 'test'), may hold values from -0.09375 to 0.09375
- down_weight: bfloat16 [8192, 4096], P('test', 'dp'), may hold values from -0.0625 to 0.0625
- in_proj: bfloat16 [4096, 64], replicated, may hold values from -0.09375 to 0.09375
- out_proj: bfloat16 [8192, 64], P('test'), may hold values from -0.0625 to 0.0625
- test_grads: bfloat16 [1024, 4096], P('test'), may hold values from -0.0234375 to 0.0234375
Outputs:
- scores: float32 [32, 1024], P('dp', 'test')
Inputs may be any that keep to these rules, and one draw needn't show every extreme that they name: The first lengths[p, s] of the 128 slots of a sequence hold tokens, the rest are padding; shorter sequences are more common, and some sequence fills all 128 slots.
All inputs are finite; a program needn't handle non-finite values.
Results may differ from a plain program's by a relative error of at most 0.0041.
Values may be sent and summed in bfloat16 or wider, within the bound.
No kernel may reach another device: no remote copies, remote signals or barrier semaphores. Data moves between devices by JAX's collectives and lax.ppermute only.
A program may use at most 64 MiB of HBM per device.

v0:
```python
import jax
import jax.numpy as jnp
from jax import lax
from jax.sharding import PartitionSpec as P


def silu_slope(gate_pre):
    sigmoid_val = jax.nn.sigmoid(gate_pre)
    return sigmoid_val * (1.0 + gate_pre * (1.0 - sigmoid_val))


def per_device(
    tokens,
    upstream,
    rewards,
    lengths,
    gate_weight,
    up_weight,
    down_weight,
    in_proj,
    out_proj,
    test_grads,
):
    features, upstream_full = (
        lax.all_gather(tokens, "test", axis=1, tiled=True),
        lax.all_gather(upstream, "test", axis=1, tiled=True),
    )
    row_count = features.shape[0]
    pair_count = lengths.shape[0]
    slot_count = row_count // (2 * pair_count)
    position = lax.broadcasted_iota(jnp.int32, (pair_count, 2, slot_count), 2)
    side_index = lax.broadcasted_iota(jnp.int32, (pair_count, 2, slot_count), 1)
    live_mask = (position < lengths[:, :, None]).astype(jnp.float32)
    side_sign = jnp.where(side_index == 1, 1.0, -1.0).astype(jnp.float32)
    pair_coef = jax.nn.sigmoid(rewards[:, 1] - rewards[:, 0])
    row_scale = (pair_coef[:, None, None] * side_sign * live_mask).reshape(row_count, 1)
    columns = features
    gate_pre = jnp.dot(
        columns,
        lax.all_gather(gate_weight, "dp", axis=0, tiled=True),
        preferred_element_type=jnp.float32,
    )
    up_pre = jnp.dot(
        columns,
        lax.all_gather(up_weight, "dp", axis=0, tiled=True),
        preferred_element_type=jnp.float32,
    )
    columns = upstream_full
    back_grad = lax.dot_general(
        columns,
        lax.all_gather(down_weight, "dp", axis=1, tiled=True),
        (((1,), (1,)), ((), ())),
        preferred_element_type=jnp.float32,
    )
    gate_grad = (row_scale * back_grad * up_pre * silu_slope(gate_pre)).astype(jnp.bfloat16)
    in_factor = jnp.dot(features, in_proj, preferred_element_type=jnp.float32).reshape(
        pair_count, 2 * slot_count, -1
    )
    out_partial = jnp.dot(gate_grad, out_proj, preferred_element_type=jnp.float32).reshape(
        pair_count, 2 * slot_count, -1
    )
    out_factor = lax.psum(out_partial, "test")
    pair_grads = jnp.einsum("prk,prj->pkj", in_factor, out_factor, precision=lax.Precision.HIGHEST)
    flat_grads = pair_grads.reshape(pair_count, -1).astype(jnp.bfloat16)
    return lax.dot_general(
        flat_grads, test_grads, (((1,), (1,)), ((), ())), preferred_element_type=jnp.float32
    )


def solution(mesh):
    placed = (
        P("dp", "test"),
        P("dp", "test"),
        P("dp", None),
        P("dp", None),
        P("dp", "test"),
        P("dp", "test"),
        P("test", "dp"),
        P(),
        P("test", None),
        P("test", None),
    )
    return jax.shard_map(
        per_device, mesh=mesh, in_specs=placed, out_specs=P("dp", "test"), check_vma=False
    )
```

profile of v0, /device:TPU:1, one launch (start us, length us, event | category | flops | bytes accessed | tf_op | source)
XLA Modules:
  0.0 738.4 jit_solution(75771577556798764)
XLA Ops:
  6.5 0.0 copy-start
  6.5 0.0 all-gather.6.cloned.1.call-start
  6.5 0.7 all-gather.6.cloned.1.call-update
  7.3 0.0 all-gather.14.cloned.1.call-start
  7.3 0.7 all-gather.14.cloned.1.call-update
  8.0 0.0 all-gather.8.cloned.1.call-start
  8.1 0.7 all-gather.8.cloned.1.call-update
  8.7 0.0 all-gather.10.cloned.1.call-start
  8.8 0.5 all-gather.10.cloned.1.call-update
  9.3 0.0 all-gather.12.cloned.1.call-start
  9.4 0.5 all-gather.12.cloned.1.call-update
  9.9 0.0 all-reduce.2.cloned.1.call-start
  10.0 1.4 fusion.14
  12.8 0.1 iota.18
  12.8 0.7 lt.16
  13.6 46.7 %all-gather.6.cloned.1.call-done = bf16[256,4096]{1,0:T(8,128)(2,1)} async-done(((bf16[256,256]{1,0:T(8,128)(2,1)}), bf16[256,4096]{1,0:T(8,128)(2,1)}) %all-gather.6.cloned.1.call-update) | async-done | bytes 2097168 | tf_op jit(solution)/shard_map/all_gather | solution.py:25
  60.3 158.9 %all-gather.14.cloned.1.call-done = bf16[4096,512]{1,0:T(8,128)(2,1)} async-done(((bf16[128,512]{1,0:T(8,128)(2,1)}), bf16[4096,512]{1,0:T(8,128)(2,1)}) %all-gather.14.cloned.1.call-update) | async-done | bytes 4194320 | tf_op jit(solution)/shard_map/all_gather | solution.py:40
  219.2 4.9 fusion.16
  224.1 0.0 copy-start.1
  224.1 0.0 copy-start.3
  224.1 45.5 %all-gather.8.cloned.1.call-done = bf16[256,4096]{1,0:T(8,128)(2,1)} async-done(((bf16[256,256]{1,0:T(8,128)(2,1)}), bf16[256,4096]{1,0:T(8,128)(2,1)}) %all-gather.8.cloned.1.call-update) | async-done | bytes 2097168 | tf_op jit(solution)/shard_map/all_gather | solution.py:26
  269.5 160.3 %all-gather.10.cloned.1.call-done = bf16[512,4096]{1,0:T(8,128)(2,1)} async-done(((bf16[512,128]{1,0:T(8,128)(2,1)}), bf16[512,4096]{1,0:T(8,128)(2,1)}) %all-gather.10.cloned.1.call-update) | async-done | bytes 4194320 | tf_op jit(solution)/shard_map/all_gather | solution.py:51
  429.9 4.1 convolution_multiply_fusion.1
  434.0 157.3 %all-gather.12.cloned.1.call-done = bf16[4096,512]{1,0:T(8,128)(2,1)} async-done(((bf16[128,512]{1,0:T(8,128)(2,1)}), bf16[4096,512]{1,0:T(8,128)(2,1)}) %all-gather.12.cloned.1.call-update) | async-done | bytes 4194320 | tf_op jit(solution)/shard_map/all_gather | solution.py:45
  591.2 0.0 copy-done.1
  591.2 0.0 copy-done.3
  591.3 4.4 fusion.2
  595.7 0.0 copy-start.2
  595.7 0.0 all-reduce.2.cloned.1.call-update
  595.7 0.0 copy-done
  595.7 0.7 fusion.15
  596.4 133.0 %all-reduce.2.cloned.1.call-done = f32[256,64]{1,0:T(8,128)} async-done(((f32[256,64]{1,0:T(8,128)}), f32[256,64]{1,0:T(8,128)}) %all-reduce.2.cloned.1.call-update) | async-done | bytes 65552 | tf_op jit(solution)/shard_map/psum | solution.py:62
  729.4 1.3 convolution_convert_fusion
  730.7 0.1 reshape.73
  730.7 0.0 copy-done.2
  730.8 0.8 fusion.17
  (2 shorter events, 0.0 us)
Async XLA Ops:
  6.5 589.1 %copy-start = (bf16[4096,64]{0,1:T(8,128)(2,1)S(1)}, bf16[4096,64]{0,1:T(8,128)(2,1)}, u32[]{:S(2)}) copy-start(bf16[4096,64]{0,1:T(8,128)(2,1)} %param.17) | copy-start | bytes 1572868
  6.5 53.7 %all-gather.6.cloned.1.call-start = ((), (), s32[]{:S(2)}) async-start(), calls=%async_computation | async-start | bytes 2228224 | tf_op jit(solution)/shard_map/all_gather | solution.py:25
  7.3 212.0 %all-gather.14.cloned.1.call-start = ((), (), s32[]{:S(2)}) async-start(), calls=%async_computation.4 | async-start | bytes 4325376 | tf_op jit(solution)/shard_map/all_gather | solution.py:40
  8.0 261.5 %all-gather.8.cloned.1.call-start = ((), (), s32[]{:S(2)}) async-start(), calls=%async_computation.1 | async-start | bytes 2228224 | tf_op jit(solution)/shard_map/all_gather | solution.py:26
  8.7 421.1 %all-gather.10.cloned.1.call-start = ((), (), s32[]{:S(2)}) async-start(), calls=%async_computation.2 | async-start | bytes 4325376 | tf_op jit(solution)/shard_map/all_gather | solution.py:51
  9.3 581.9 %all-gather.12.cloned.1.call-start = ((), (), s32[]{:S(2)}) async-start(), calls=%async_computation.3 | async-start | bytes 4325376 | tf_op jit(solution)/shard_map/all_gather | solution.py:45
  9.9 719.5 %all-reduce.2.cloned.1.call-start = ((), (), s32[]{:S(2)}) async-start(), calls=%async_computation.5 | async-start | bytes 262144 | tf_op jit(solution)/shard_map/psum | solution.py:62
  224.1 367.2 %copy-start.1 = (bf16[256,4096]{1,0:T(8,128)(2,1)S(1)}, bf16[256,4096]{1,0:T(8,128)(2,1)}, u32[]{:S(2)}) copy-start(bf16[256,4096]{1,0:T(8,128)(2,1)} %all-gather.6.cloned.1.call-done) | copy-start | bytes 6291460
  224.1 367.2 %copy-start.3 = (bf16[512,64]{0,1:T(8,128)(2,1)S(1)}, bf16[512,64]{0,1:T(8,128)(2,1)}, u32[]{:S(2)}) copy-start(bf16[512,64]{0,1:T(8,128)(2,1)} %param.18) | copy-start | bytes 196612
  595.7 135.1 %copy-start.2 = (bf16[64,4096]{1,0:T(8,128)(2,1)S(1)}, bf16[64,4096]{1,0:T(8,128)(2,1)}, u32[]{:S(2)}) copy-start(bf16[64,4096]{1,0:T(8,128)(2,1)} %param.19) | copy-start | bytes 1572868
Sparse Core Ops, SparseCore 0:
  9.4 50.8 all-gather.5
  63.4 155.7 all-gather.13
  221.3 48.2 all-gather.7
  272.3 157.5 all-gather.9
  432.8 158.3 all-gather.11
  595.8 133.5 all-reduce.1
where the time goes:
time: 739 us; the launch traced here: 738 us
  waiting for transfers between devices  705 us (95%)
  matrix products  16.1 us (2%)
  between operations  14.9 us (2%)
    all_gather x1, waiting for transfers between devices, per_device(): lax.all_gather(down_weight, 'dp', axis=1, tiled=True)  160 us
    all_gather x1, waiting for transfers between devices, per_device(): lax.all_gather(gate_weight, 'dp', axis=0, tiled=True)  159 us
    all_gather x1, waiting for transfers between devices, per_device(): lax.all_gather(up_weight, 'dp', axis=0, tiled=True)  157 us
    psum x1, waiting for transfers between devices, per_device(): out_factor = lax.psum(out_partial, 'test')  133 us
    all_gather x1, waiting for transfers between devices, per_device(): lax.all_gather(tokens, 'test', axis=1, tiled=True)  46.7 us
    all_gather x1, waiting for transfers between devices, per_device(): lax.all_gather(upstream, 'test', axis=1, tiled=True)  45.5 us
  transfers between devices with their start and end apart: 6, of which 6 were waited for; matrix products, arithmetic and copies ran while one was open for 2% of the time, Pallas kernels for 0%

commit v1 on v0

v1 whole, which is shorter than its diff:
```python
import jax
import jax.numpy as jnp
from jax import lax
from jax.experimental import pallas as pl
from jax.experimental.pallas import tpu as pltpu
from jax.sharding import Mesh
from jax.sharding import PartitionSpec as P

SIZES = (2, 16, 4, 2, 2)
NAMES = ("xh", "z", "y", "xl", "c")
DP = ("xh", "z")
TEST = ("y", "xl", "c")
PLANE = ("xh", "y", "xl")
F32 = jnp.float32
BF16 = jnp.bfloat16


def layer_kernel(core_ref, own_ref, other_ref, weight_ref, in_ref, scale_ref, out_ref, pair_ref, pre, back, infac):
    step = pl.program_id(0)
    core = core_ref[0]

    @pl.when(step == 0)
    def _():
        pre[...] = jnp.zeros_like(pre)
        back[...] = jnp.zeros_like(back)
        infac[...] = jnp.zeros_like(infac)

    for pair in range(2):
        rows = slice(pair * 256, pair * 256 + 256)
        for ref, which in ((own_ref, core), (other_ref, 1 - core)):
            base = pl.multiple_of(which * 512, 512)

            def columns(kind):
                return jnp.concatenate(
                    [
                        ref[pair * 2 + half, 0, kind * 256 : kind * 256 + 256, odd * 128 : odd * 128 + 128]
                        for odd in range(2)
                        for half in range(2)
                    ],
                    axis=1,
                )

            features = columns(0)
            pre[rows, :] += jnp.dot(features, weight_ref[pl.ds(base, 512), :512], preferred_element_type=F32)
            infac[rows, :] += jnp.dot(features, in_ref[pl.ds(base, 512), :], preferred_element_type=F32)
            back[rows, :] += jnp.dot(columns(1), weight_ref[pl.ds(base, 512), 512:], preferred_element_type=F32)

    @pl.when(step == pl.num_programs(0) - 1)
    def _():
        gate = pre[:, :256]
        sig = jax.nn.sigmoid(gate)
        slope = sig * (1.0 + gate * (1.0 - sig))
        grad = (scale_ref[:, :1] * back[...] * pre[:, 256:] * slope).astype(BF16)
        out = jnp.dot(grad, out_ref[...], preferred_element_type=F32)
        lane = lax.broadcasted_iota(jnp.int32, (32, 128), 1)
        for pair in range(2):
            rows = slice(pair * 256, pair * 256 + 256)
            mat = lax.dot_general(
                infac[rows, :], out[rows, :], (((0,), (0,)), ((), ())),
                precision=lax.Precision.HIGHEST, preferred_element_type=F32,
            )
            pair_ref[pair] = jnp.where(lane < 64, mat[:32], mat[32:64])


def layer(core, own, other, weights, in_rows, scale, out_twice):
    return pl.pallas_call(
        layer_kernel,
        grid_spec=pltpu.PrefetchScalarGridSpec(
            num_scalar_prefetch=1,
            grid=(4,),
            in_specs=[
                pl.BlockSpec((4, 1, 512, 256), lambda q, c: (0, q, 0, 0)),
                pl.BlockSpec((4, 1, 512, 256), lambda q, c: (0, q, 0, 0)),
                pl.BlockSpec((1024, 768), lambda q, c: (q, 0)),
                pl.BlockSpec((1024, 64), lambda q, c: (q, 0)),
                pl.BlockSpec((512, 128), lambda q, c: (0, 0)),
                pl.BlockSpec((256, 128), lambda q, c: (0, 0)),
            ],
            out_specs=pl.BlockSpec((2, 32, 128), lambda q, c: (0, 0, 0)),
            scratch_shapes=[
                pltpu.VMEM((512, 512), F32),
                pltpu.VMEM((512, 256), F32),
                pltpu.VMEM((512, 64), F32),
            ],
        ),
        out_shape=jax.ShapeDtypeStruct((2, 32, 128), F32),
        compiler_params=pltpu.CompilerParams(vmem_limit_bytes=40 * 1024 * 1024),
        cost_estimate=pl.CostEstimate(flops=2 * 512 * 4096 * 832, bytes_accessed=15 * 1024 * 1024, transcendentals=131072),
    )(core, own, other, weights, in_rows, scale, out_twice)


def per_device(
    tokens, upstream, rewards, lengths, gate_weight, up_weight, down_weight, in_proj, out_proj, test_grads
):
    xh = lax.axis_index("xh")
    core = lax.axis_index("c")
    swap = [(0, 1), (1, 0)]

    halves = [
        jnp.concatenate(
            [gate_weight[:, lo : lo + 256], up_weight[:, lo : lo + 256], down_weight[lo : lo + 256].T], axis=1
        )
        for lo in (0, 256)
    ]
    mine = jnp.where(xh == 0, halves[0], halves[1])
    theirs = lax.ppermute(jnp.where(xh == 0, halves[1], halves[0]), "xh", swap)
    block = jnp.where(xh == 0, jnp.stack([mine, theirs]), jnp.stack([theirs, mine]))
    weights = lax.all_gather(block, "z").reshape(4096, 768)

    nothing = theirs[:1, :256] * 0
    acts = jnp.concatenate([tokens, upstream], axis=0) + nothing
    own = lax.all_to_all(jnp.broadcast_to(acts[None], (16, 512, 256)), PLANE, 0, 0)
    other = lax.ppermute(own, "c", swap)

    position = lax.broadcasted_iota(jnp.int32, (2, 128), 1)
    side = lax.broadcasted_iota(jnp.int32, (2, 128), 0)
    coef = jax.nn.sigmoid(rewards[0, 1] - rewards[0, 0])
    live = (position < lengths.reshape(2, 1)).astype(F32)
    scale = (coef * jnp.where(side == 1, 1.0, -1.0).astype(F32) * live).reshape(2, 128)
    scale_other = lax.ppermute(scale, "xh", swap)
    scale = jnp.where(xh == 0, jnp.stack([scale, scale_other]), jnp.stack([scale_other, scale]))
    scale = jnp.broadcast_to(scale.reshape(512, 1), (512, 128))

    in_rows = in_proj.reshape(2, 16, 128, 32, 2).transpose(1, 0, 2, 4, 3).reshape(4096, 64)
    out_half = jnp.where(xh == 0, out_proj[:256], out_proj[256:])
    out_twice = jnp.concatenate([out_half, out_half], axis=1)

    pairs = layer(
        core.reshape(1).astype(jnp.int32),
        own.reshape(4, 4, 512, 256),
        other.reshape(4, 4, 512, 256),
        weights,
        in_rows,
        scale,
        out_twice,
    )
    spread = jnp.broadcast_to(pairs[:, None], (2, 16, 32, 128)).reshape(32, 32, 128)
    parts = lax.all_to_all(spread, ("xh",) + TEST, 0, 0)
    flat = jnp.sum(parts, axis=0).astype(BF16).reshape(1, 4096)
    return lax.dot_general(flat, test_grads, (((1,), (1,)), ((), ())), preferred_element_type=F32)


def solution(mesh):
    fine = Mesh(mesh.devices.reshape(SIZES), NAMES)
    placed = (
        P(DP, TEST),
        P(DP, TEST),
        P(DP, None),
        P(DP, None),
        P(DP, TEST),
        P(DP, TEST),
        P(TEST, DP),
        P(),
        P(TEST, None),
        P(TEST, None),
    )
    return jax.shard_map(per_device, mesh=fine, in_specs=placed, out_specs=P(DP, TEST), check_vma=False)
```

time: 739 us -> 147 us (0.20)
  waiting for transfers between devices: 705 us -> 23.7 us
  blocking collectives: 0 us -> 77.7 us
  matrix products: 16.1 us -> 0.76 us
  starting transfers between devices: 0.19 us -> 13.7 us
  Pallas kernels: 0 us -> 8.86 us
    all_gather x5 -> x1, waiting for transfers between devices: 569 us -> 19.5 us  [per_device(): weights = lax.all_gather(block, 'z').reshape(4096, 768)]
    psum x1 -> x0, waiting for transfers between devices: 133 us -> none  [per_device(): out_factor = lax.psum(out_partial, 'test')]
    all_to_all x0 -> x2, blocking collectives: none -> 77.7 us  [the longest x1 56.8 us: per_device(): lax.all_to_all(jnp.broadcast_to(acts[None], (16, 512, 256)), PLANE, 0, 0)]
    dot_general x6 -> x1, matrix products: 16.1 us -> 0.76 us  [per_device(): lax.dot_general(flat, test_grads, (((1,), (1,)), ((), ())), preferred_ele...]
    ppermute x0 -> x3, starting transfers between devices: none -> 13.7 us  [the longest x1 5.48 us: per_device(): theirs = lax.ppermute(jnp.where(xh == 0, halves[1], halves[0]), 'xh', swap)]
    pallas_call x0 -> x1, Pallas kernels: none -> 8.86 us  [layer(): pl.pallas_call(layer_kernel, grid_spec=pltpu.PrefetchScalarGridSpec(num_s...]
  transfers between devices with their start and end apart: 6 -> 4, of which waited for: 6 -> 3; matrix products, arithmetic and copies ran while one was open for 2% -> 3% of each run, Pallas kernels for 0% -> 0%
where the time goes in v1:
time: 147 us
  blocking collectives  77.7 us (53%)
  waiting for transfers between devices  23.7 us (16%)
  between operations  15 us (10%)
  starting transfers between devices  13.7 us (9%)
  Pallas kernels  8.86 us (6%)
  local copies, waits for them, and re-layouts  4.95 us (3%)
  other arithmetic  2.27 us (2%)
    all_to_all x1, blocking collectives, per_device(): lax.all_to_all(jnp.broadcast_to(acts[None], (16, 512, 256)), PLANE, 0, 0)  56.8 us
    all_to_all x1, blocking collectives, per_device(): parts = lax.all_to_all(spread, ('xh',) + TEST, 0, 0)  20.9 us
    all_gather x1, waiting for transfers between devices, per_device(): weights = lax.all_gather(block, 'z').reshape(4096, 768)  19.5 us
    pallas_call x1, Pallas kernels, layer(): pl.pallas_call(layer_kernel, grid_spec=pltpu.PrefetchScalarGridSpec(num_s...  8.86 us
    ppermute x1, starting transfers between devices, per_device(): theirs = lax.ppermute(jnp.where(xh == 0, halves[1], halves[0]), 'xh', swap)  5.48 us
    ppermute x1, starting transfers between devices, per_device(): other = lax.ppermute(own, 'c', swap)  5.48 us
    ppermute x1, waiting for transfers between devices, per_device(): theirs = lax.ppermute(jnp.where(xh == 0, halves[1], halves[0]), 'xh', swap)  2.99 us
  transfers between devices with their start and end apart: 4, of which 3 were waited for; matrix products, arithmetic and copies ran while one was open for 3% of the time, Pallas kernels for 0%

profile of v1, /device:TPU:1, one launch (start us, length us, event | category | flops | bytes accessed | tf_op | source)
XLA Modules:
  0.0 147.0 jit_solution(16733700780646386214)
XLA Ops:
  6.5 0.0 copy-start
  6.5 0.0 all-gather.2.cloned.1.call-start
  6.5 0.9 fusion.3
  7.5 0.1 copy.41
  7.6 0.1 copy.40
  7.7 1.0 slice_bitcast_fusion.2
  8.7 0.1 maximum_select_fusion.1
  8.8 5.5 %collective-permute-start = (bf16[128,768]{1,0:T(8,128)(2,1)S(1)}, bf16[128,768]{1,0:T(8,128)(2,1)S(1)}, u32[]{:S(2)}, u32[]{:S(2)}) collective-permute-start(bf16[128,768]{1,0:T(8,128)(2,1)S(1)} %maximum_select_fusion.1), channel_id=1, source_target_pairs={{0,256},{256,0},{1,257},{257,1},{2,258},{258,2},{3,259},{259,3},{4... | collective-permute-start | bytes 589832 | tf_op jit(solution)/shard_map/ppermute | solution.py:106
  14.2 0.1 fusion
  14.3 3.0 %collective-permute-done = bf16[128,768]{1,0:T(8,128)(2,1)S(1)} collective-permute-done((bf16[128,768]{1,0:T(8,128)(2,1)S(1)}, bf16[128,768]{1,0:T(8,128)(2,1)S(1)}, u32[]{:S(2)}, u32[]{:S(2)}) %collective-permute-start) | collective-permute-done | bytes 196640 | tf_op jit(solution)/shard_map/ppermute | solution.py:106
  17.3 0.8 maximum_select_fusion
  18.1 0.0 all-gather.2.cloned.1.call-update
  18.2 1.0 maximum_add_fusion
  19.2 0.4 broadcast_in_dim.14
  19.6 0.0 copy-start.3
  19.6 0.0 copy-start.4
  19.6 0.0 copy-start.2
  19.6 0.0 copy-start.1
  19.6 56.8 %all_to_all.10 = bf16[16,512,256]{2,1,0:T(8,128)(2,1)} all-to-all(bf16[16,512,256]{2,1,0:T(8,128)(2,1)S(1)} %broadcast_in_dim.14), channel_id=1, replica_groups=mesh['xh'=2,'z'=16,'y'=4,'xl'=2,'c'=2] {'xh','y','xl'}, dimensions={0} | all-to-all | bytes 8388608 | tf_op jit(solution)/shard_map/all_to_all | solution.py:112
  76.5 5.5 %collective-permute-start.1 = (bf16[16,512,256]{2,1,0:T(8,128)(2,1)}, bf16[16,512,256]{2,1,0:T(8,128)(2,1)}, u32[]{:S(2)}, u32[]{:S(2)}) collective-permute-start(bf16[16,512,256]{2,1,0:T(8,128)(2,1)} %all_to_all.10), channel_id=1, source_target_pairs={{0,1},{1,0},{2,3},{3,2},{4,5},{5,4},{6,7},{7,6},{8,9},{9,8},{10,11... | collective-permute-start | bytes 12582920 | tf_op jit(solution)/shard_map/ppermute | solution.py:113
  82.0 0.0 copy-done.3
  82.0 0.6 fusion.5
  84.0 0.0 copy-done.4
  84.0 0.1 compare_select_fusion
  84.0 2.7 %collective-permute-start.2 = (f32[2,128]{1,0:T(2,128)S(1)}, f32[2,128]{1,0:T(2,128)S(1)}, u32[]{:S(2)}, u32[]{:S(2)}) collective-permute-start(f32[2,128]{1,0:T(2,128)S(1)} %compare_select_fusion), channel_id=1, source_target_pairs={{0,256},{256,0},{1,257},{257,1},{2,258},{258,2},{3,259},{259,3},{4... | collective-permute-start | bytes 3080 | tf_op jit(solution)/shard_map/ppermute | solution.py:120
  86.8 0.0 copy-done.2
  86.8 0.1 copy.43
  86.9 0.1 copy.42
  87.0 0.1 compare_select_fusion.2
  87.1 0.1 pad_maximum_fusion.out_ref
  87.2 0.0 copy-done.1
  87.2 0.1 copy.44
  87.3 0.4 copy.46
  87.8 0.4 reshape.367
  88.2 0.5 copy.39.in_ref
  88.6 1.3 collective-permute-done.2
  89.9 0.0 collective-permute-done.1
  89.9 19.5 %all-gather.2.cloned.1.call-done = bf16[16,2,128,768]{3,2,1,0:T(8,128)(2,1)} async-done(((bf16[1,2,128,768]{3,2,1,0:T(8,128)(2,1)}), bf16[16,2,128,768]{3,2,1,0:T(8,128)(2,1)}) %all-gather.2.cloned.1.call-update) | async-done | bytes 6291472 | tf_op jit(solution)/shard_map/all_gather | solution.py:108
  109.4 0.1 broadcast_in_dim.28.scale_ref
  109.5 8.9 %shard_map.103 = f32[2,32,128]{2,1,0:T(8,128)S(1)} custom-call(s32[1]{0:T(128)} %bitcast.core_ref, bf16[4,4,512,256]{3,2,1,0:T(8,128)(2,1)} %bitcast.3.own_ref, bf16[4,4,512,256]{3,2,1,0:T(8,128)(2,1)} %bitcast.4.other_ref, bf16[4096,768]{1,0:T(8,128)(2,1)} %bitcast.42, bf16[4096,64]{1,0:T(8,128)(2,1)S(1)} %copy.39.in_ref, ...), custom_call_target="tpu_custom_call" | custom-call | flops 3489660928 | bytes 15728640 | tf_op jit(solution)/shard_map/pallas_call | solution.py:66
  118.4 0.1 broadcast_in_dim.29
  118.4 20.9 %all_to_all.11 = f32[32,32,128]{2,1,0:T(8,128)S(1)} all-to-all(f32[32,32,128]{2,1,0:T(8,128)S(1)} %bitcast.44), channel_id=1, replica_groups=mesh['xh'=2,'z'=16,'y'=4,'xl'=2,'c'=2] {'xh','y','xl','c'}, dimensions={0} | all-to-all | bytes 1048576 | tf_op jit(solution)/shard_map/all_to_all | solution.py:138
  139.4 0.0 copy-done
  139.4 0.8 fusion.6
  (7 shorter events, 0.1 us)
Async XLA Ops:
  6.5 132.8 %copy-start = (bf16[64,4096]{1,0:T(8,128)(2,1)S(1)}, bf16[64,4096]{1,0:T(8,128)(2,1)}, u32[]{:S(2)}) copy-start(bf16[64,4096]{1,0:T(8,128)(2,1)} %param.19) | copy-start | bytes 1572868
  6.5 102.8 %all-gather.2.cloned.1.call-start = ((), (), s32[]{:S(2)}) async-start(), calls=%async_computation.2 | async-start | bytes 6684672 | tf_op jit(solution)/shard_map/all_gather | solution.py:108
  8.8 8.5 %collective-permute-start = (bf16[128,768]{1,0:T(8,128)(2,1)S(1)}, bf16[128,768]{1,0:T(8,128)(2,1)S(1)}, u32[]{:S(2)}, u32[]{:S(2)}) collective-permute-start(bf16[128,768]{1,0:T(8,128)(2,1)S(1)} %maximum_select_fusion.1), channel_id=1, source_target_pairs={{0,256},{256,0},{1,257},{257,1},{2,258},{258,2},{3,259},{259,3},{4... | collective-permute-start | bytes 589832 | tf_op jit(solution)/shard_map/ppermute | solution.py:106
  19.6 62.4 %copy-start.3 = (f32[1,2]{1,0:T(1,128)S(1)}, f32[1,2]{1,0:T(1,128)}, u32[]{:S(2)}) copy-start(f32[1,2]{1,0:T(1,128)} %param.12) | copy-start | bytes 28
  19.6 64.4 %copy-start.4 = (s32[1,2]{1,0:T(1,128)S(1)}, s32[1,2]{1,0:T(1,128)}, u32[]{:S(2)}) copy-start(s32[1,2]{1,0:T(1,128)} %param.13) | copy-start | bytes 28
  19.6 67.2 %copy-start.2 = (bf16[512,64]{0,1:T(8,128)(2,1)S(1)}, bf16[512,64]{0,1:T(8,128)(2,1)}, u32[]{:S(2)}) copy-start(bf16[512,64]{0,1:T(8,128)(2,1)} %param.18) | copy-start | bytes 196612
  19.6 67.6 %copy-start.1 = (bf16[4096,64]{0,1:T(8,128)(2,1)S(1)}, bf16[4096,64]{0,1:T(8,128)(2,1)}, u32[]{:S(2)}) copy-start(bf16[4096,64]{0,1:T(8,128)(2,1)} %param.17) | copy-start | bytes 1572868
  76.5 13.4 %collective-permute-start.1 = (bf16[16,512,256]{2,1,0:T(8,128)(2,1)}, bf16[16,512,256]{2,1,0:T(8,128)(2,1)}, u32[]{:S(2)}, u32[]{:S(2)}) collective-permute-start(bf16[16,512,256]{2,1,0:T(8,128)(2,1)} %all_to_all.10), channel_id=1, source_target_pairs={{0,1},{1,0},{2,3},{3,2},{4,5},{5,4},{6,7},{7,6},{8,9},{9,8},{10,11... | collective-permute-start | bytes 12582920 | tf_op jit(solution)/shard_map/ppermute | solution.py:113
  84.0 5.9 %collective-permute-start.2 = (f32[2,128]{1,0:T(2,128)S(1)}, f32[2,128]{1,0:T(2,128)S(1)}, u32[]{:S(2)}, u32[]{:S(2)}) collective-permute-start(f32[2,128]{1,0:T(2,128)S(1)} %compare_select_fusion), channel_id=1, source_target_pairs={{0,256},{256,0},{1,257},{257,1},{2,258},{258,2},{3,259},{259,3},{4... | collective-permute-start | bytes 3080 | tf_op jit(solution)/shard_map/ppermute | solution.py:120
Sparse Core Ops, SparseCore 0:
  18.3 91.0 all-gather.1

commit v2 on v1

v2 whole, which is shorter than its diff:
```python
import jax
import jax.numpy as jnp
from jax import lax
from jax.experimental import pallas as pl
from jax.experimental.pallas import tpu as pltpu
from jax.sharding import Mesh
from jax.sharding import PartitionSpec as P

SIZES = (2, 16, 4, 2, 2)
NAMES = ("xh", "z", "y", "xl", "c")
DP = ("xh", "z")
TEST = ("y", "xl", "c")
PLANE = ("xh", "y", "xl")
F32 = jnp.float32
BF16 = jnp.bfloat16
MIB = 1024 * 1024


def pack_kernel(place, gate_ref, up_ref, down_ref, mine_ref, send_ref):
    xh = place[0]
    for half, ref in ((xh, mine_ref), (1 - xh, send_ref)):
        units = pl.ds(pl.multiple_of(half * 256, 256), 256)
        ref[:, :256] = gate_ref[:, units]
        ref[:, 256:512] = up_ref[:, units]
        ref[:, 512:] = down_ref[units, :].T


def pack(place, gate_weight, up_weight, down_weight):
    here = pl.BlockSpec(memory_space=pltpu.VMEM)
    return pl.pallas_call(
        pack_kernel,
        in_specs=[pl.BlockSpec(memory_space=pltpu.SMEM), here, here, here],
        out_specs=[here, here],
        out_shape=[jax.ShapeDtypeStruct((128, 768), BF16)] * 2,
        compiler_params=pltpu.CompilerParams(vmem_limit_bytes=8 * MIB),
        cost_estimate=pl.CostEstimate(flops=0, bytes_accessed=768 * 1024, transcendentals=0),
    )(place, *(pltpu.with_memory_space_constraint(each, pltpu.HBM) for each in (gate_weight, up_weight, down_weight)))


def order_kernel(place, own_ref, other_ref, in_ref, rows_ref, infac_ref):
    core = place[2]
    infac = jnp.zeros((512, 64), F32)
    for plane in range(16):
        ours = (plane // 2) % 2 == core
        lanes = slice(plane % 2 * 128, plane % 2 * 128 + 128)
        for half in range(2):
            into = slice(plane % 8 * 256 + half * 128, plane % 8 * 256 + half * 128 + 128)
            for pair in range(2):
                for kind in range(2):
                    slots = slice(kind * 256, kind * 256 + 256)
                    rows_ref[plane // 8, kind, pair * 256 : pair * 256 + 256, into] = jnp.where(
                        ours,
                        own_ref[pair, half, plane // 4, slots, lanes],
                        other_ref[pair, half, plane // 4, slots, lanes],
                    )
        in_rows = jnp.concatenate(
            [in_ref[(half * 16 + plane) * 128 : (half * 16 + plane) * 128 + 128, :] for half in range(2)], axis=0
        )
        infac += jnp.dot(
            rows_ref[plane // 8, 0, :, plane % 8 * 256 : plane % 8 * 256 + 256], in_rows, preferred_element_type=F32
        )
    row = lax.broadcasted_iota(jnp.int32, (64, 64), 0)
    column = lax.broadcasted_iota(jnp.int32, (64, 64), 1)
    even_first = (row == jnp.where(column < 32, 2 * column, 2 * column - 63)).astype(F32)
    infac_ref[...] = jnp.dot(infac, even_first, precision=lax.Precision.HIGHEST, preferred_element_type=F32)


def order(place, own, other, in_proj):
    here = pl.BlockSpec(memory_space=pltpu.VMEM)
    return pl.pallas_call(
        order_kernel,
        in_specs=[pl.BlockSpec(memory_space=pltpu.SMEM), here, here, here],
        out_specs=[here, here],
        out_shape=[jax.ShapeDtypeStruct((2, 2, 512, 2048), BF16), jax.ShapeDtypeStruct((512, 64), F32)],
        compiler_params=pltpu.CompilerParams(vmem_limit_bytes=24 * MIB),
        cost_estimate=pl.CostEstimate(flops=2 * 512 * 4096 * 64, bytes_accessed=17 * MIB, transcendentals=0),
    )(place, own, other, in_proj)


def layer_kernel(rows_ref, weight_ref, infac_ref, scale_ref, out_ref, pair_ref, pre, back):
    step = pl.program_id(0)
    one = jnp.dot(rows_ref[0, 0], weight_ref[:, :512], preferred_element_type=F32)
    two = jnp.dot(rows_ref[0, 1], weight_ref[:, 512:], preferred_element_type=F32)

    @pl.when(step == 0)
    def _():
        pre[...] = one
        back[...] = two

    @pl.when(step > 0)
    def _():
        pre[...] += one
        back[...] += two

    @pl.when(step == pl.num_programs(0) - 1)
    def _():
        gate = pre[:, :256]
        sig = jax.nn.sigmoid(gate)
        slope = sig * (1.0 + gate * (1.0 - sig))
        grad = (scale_ref[:, :1] * back[...] * pre[:, 256:] * slope).astype(BF16)
        out = jnp.dot(grad, out_ref[...], preferred_element_type=F32)
        lane = lax.broadcasted_iota(jnp.int32, (32, 128), 1)
        for pair in range(2):
            slots = slice(pair * 256, pair * 256 + 256)
            mat = lax.dot_general(
                infac_ref[slots, :], out[slots, :], (((0,), (0,)), ((), ())),
                precision=lax.Precision.HIGHEST, preferred_element_type=F32,
            )
            pair_ref[pair] = jnp.where(lane < 64, mat[:32], mat[32:64]).astype(BF16)


def layer(rows, weights, infac, scale, out_twice):
    here = pl.BlockSpec(memory_space=pltpu.VMEM)
    rows = pltpu.with_memory_space_constraint(rows, pltpu.HBM)
    weights = pltpu.with_memory_space_constraint(weights, pltpu.HBM)
    return pl.pallas_call(
        layer_kernel,
        grid=(2,),
        in_specs=[
            pl.BlockSpec((1, 2, 512, 2048), lambda q: (q, 0, 0, 0)),
            pl.BlockSpec((2048, 768), lambda q: (q, 0)),
            here,
            here,
            here,
        ],
        out_specs=pl.BlockSpec((2, 32, 128), lambda q: (0, 0, 0)),
        out_shape=jax.ShapeDtypeStruct((2, 32, 128), BF16),
        scratch_shapes=[pltpu.VMEM((512, 512), F32), pltpu.VMEM((512, 256), F32)],
        compiler_params=pltpu.CompilerParams(vmem_limit_bytes=40 * MIB),
        cost_estimate=pl.CostEstimate(flops=2 * 512 * 4096 * 768, bytes_accessed=15 * MIB, transcendentals=131072),
    )(rows, weights, infac, scale, out_twice)


def per_device(
    tokens, upstream, rewards, lengths, gate_weight, up_weight, down_weight, in_proj, out_proj, test_grads
):
    xh, z, core = lax.axis_index("xh"), lax.axis_index("z"), lax.axis_index("c")
    place = jnp.stack([xh, z, core]).astype(jnp.int32)
    swap = [(0, 1), (1, 0)]

    mine, send = pack(place, gate_weight, up_weight, down_weight)
    theirs = lax.ppermute(send, "xh", swap)
    block = jnp.where(xh == 0, jnp.stack([mine, theirs]), jnp.stack([theirs, mine]))
    weights = lax.all_gather(block, "z").reshape(4096, 768)

    acts = jnp.concatenate([tokens, upstream], axis=0) + theirs[0, 0] * 0
    own = lax.all_to_all(jnp.broadcast_to(acts[None], (16, 512, 256)), PLANE, 0, 0).reshape(2, 2, 4, 512, 256)
    other = lax.ppermute(own, "c", swap)

    position = lax.broadcasted_iota(jnp.int32, (2, 128), 1)
    side = lax.broadcasted_iota(jnp.int32, (2, 128), 0)
    coef = jax.nn.sigmoid(rewards[0, 1] - rewards[0, 0])
    live = (position < lengths.reshape(2, 1)).astype(F32)
    scale = (coef * jnp.where(side == 1, 1.0, -1.0).astype(F32) * live).reshape(2, 128)
    scale_other = lax.ppermute(scale, "xh", swap)
    scale = jnp.where(xh == 0, jnp.stack([scale, scale_other]), jnp.stack([scale_other, scale]))
    scale = jnp.broadcast_to(scale.reshape(512, 1), (512, 128))

    out_half = jnp.where(xh == 0, out_proj[:256], out_proj[256:])
    out_twice = jnp.concatenate([out_half, out_half], axis=1)

    rows, infac = order(place, own, other, in_proj)
    pairs = layer(rows, weights, infac, scale, out_twice)
    spread = jnp.broadcast_to(pairs[:, None], (2, 16, 32, 128)).reshape(32, 32, 128)
    parts = lax.all_to_all(spread, ("xh",) + TEST, 0, 0)
    flat = jnp.sum(parts.astype(F32), axis=0).astype(BF16).reshape(1, 4096)
    return lax.dot_general(flat, test_grads, (((1,), (1,)), ((), ())), preferred_element_type=F32)


def solution(mesh):
    fine = Mesh(mesh.devices.reshape(SIZES), NAMES)
    placed = (
        P(DP, TEST),
        P(DP, TEST),
        P(DP, None),
        P(DP, None),
        P(DP, TEST),
        P(DP, TEST),
        P(TEST, DP),
        P(),
        P(TEST, None),
        P(TEST, None),
    )
    return jax.shard_map(per_device, mesh=fine, in_specs=placed, out_specs=P(DP, TEST), check_vma=False)
```

time: 147 us -> 142 us (0.966)
  waiting for transfers between devices: 23.7 us -> 12.8 us
  Pallas kernels: 8.86 us -> 16.4 us
  blocking collectives: 77.7 us -> 74.7 us
    all_gather x1, waiting for transfers between devices: 19.5 us -> 7.57 us  [per_device(): weights = lax.all_gather(block, 'z').reshape(4096, 768)]
    pallas_call x1 -> x3, Pallas kernels: 8.86 us -> 16.4 us  [the longest x1 7.85 us: layer(): pl.pallas_call(layer_kernel, grid=(2,), in_specs=[pl.BlockSpec((1, 2, 512...]
    unnamed x15, local copies, waits for them, and re-layouts: 0.56 us -> 3.96 us
    all_to_all x1, blocking collectives: 20.9 us -> 17.9 us  [per_device(): parts = lax.all_to_all(spread, ('xh',) + TEST, 0, 0)]
  transfers between devices with their start and end apart: 4 -> 4, of which waited for: 3 -> 3; matrix products, arithmetic and copies ran while one was open for 3% -> 2% of each run, Pallas kernels for 0% -> 5%
where the time goes in v2:
time: 142 us
  blocking collectives  74.7 us (53%)
  Pallas kernels  16.4 us (12%)
  between operations  15.6 us (11%)
  starting transfers between devices  13.7 us (10%)
  waiting for transfers between devices  12.8 us (9%)
  local copies, waits for them, and re-layouts  5.63 us (4%)
  other arithmetic  2.21 us (2%)
    all_to_all x1, blocking collectives, per_device(): lax.all_to_all(jnp.broadcast_to(acts[None], (16, 512, 256)), PLANE, 0, 0)  56.8 us
    all_to_all x1, blocking collectives, per_device(): parts = lax.all_to_all(spread, ('xh',) + TEST, 0, 0)  17.9 us
    pallas_call x1, Pallas kernels, layer(): pl.pallas_call(layer_kernel, grid=(2,), in_specs=[pl.BlockSpec((1, 2, 512...  7.85 us
    all_gather x1, waiting for transfers between devices, per_device(): weights = lax.all_gather(block, 'z').reshape(4096, 768)  7.57 us
    pallas_call x1, Pallas kernels, order(): pl.pallas_call(order_kernel, in_specs=[pl.BlockSpec(memory_space=pltpu.SM...  7.41 us
    ppermute x1, starting transfers between devices, per_device(): theirs = lax.ppermute(send, 'xh', swap)  5.48 us
    ppermute x1, starting transfers between devices, per_device(): other = lax.ppermute(own, 'c', swap)  5.48 us
    unnamed x15, local copies, waits for them, and re-layouts  3.96 us
  transfers between devices with their start and end apart: 4, of which 3 were waited for; matrix products, arithmetic and copies ran while one was open for 2% of the time, Pallas kernels for 5%

profile of v2, /device:TPU:1, one launch (start us, length us, event | category | flops | bytes accessed | tf_op | source)
XLA Modules:
  0.0 141.9 jit_solution(13636430153012454010)
XLA Ops:
  6.5 0.0 copy-start
  6.5 0.0 all-gather.2.cloned.1.call-start
  6.5 0.1 pad_add_fusion.place
  6.6 1.2 shard_map.103
  7.8 5.5 %collective-permute-start = (bf16[128,768]{1,0:T(8,128)(2,1)S(1)}, bf16[128,768]{1,0:T(8,128)(2,1)S(1)}, u32[]{:S(2)}, u32[]{:S(2)}) collective-permute-start(bf16[128,768]{1,0:T(8,128)(2,1)S(1)} %get-tuple-element.9), channel_id=1, source_target_pairs={{0,256},{256,0},{1,257},{257,1},{2,258},{258,2},{3,259},{259,3},{4... | collective-permute-start | bytes 589832 | tf_op jit(solution)/shard_map/ppermute | solution.py:142
  13.3 3.0 %collective-permute-done = bf16[128,768]{1,0:T(8,128)(2,1)S(1)} collective-permute-done((bf16[128,768]{1,0:T(8,128)(2,1)S(1)}, bf16[128,768]{1,0:T(8,128)(2,1)S(1)}, u32[]{:S(2)}, u32[]{:S(2)}) %collective-permute-start) | collective-permute-done | bytes 196640 | tf_op jit(solution)/shard_map/ppermute | solution.py:142
  16.3 0.8 maximum_select_fusion
  17.1 0.0 all-gather.2.cloned.1.call-update
  17.2 0.5 slice.20
  18.3 1.0 maximum_add_fusion
  19.4 0.4 broadcast_in_dim.14
  19.8 0.0 copy-start.4
  19.8 0.0 copy-start.5
  19.8 0.0 copy-start.3
  19.8 0.0 copy-start.2
  19.8 56.8 %all_to_all.10 = bf16[16,512,256]{2,1,0:T(8,128)(2,1)} all-to-all(bf16[16,512,256]{2,1,0:T(8,128)(2,1)S(1)} %broadcast_in_dim.14), channel_id=1, replica_groups=mesh['xh'=2,'z'=16,'y'=4,'xl'=2,'c'=2] {'xh','y','xl'}, dimensions={0} | all-to-all | bytes 8388608 | tf_op jit(solution)/shard_map/all_to_all | solution.py:147
  76.7 5.5 %collective-permute-start.1 = (bf16[2,2,4,512,256]{4,3,2,1,0:T(8,128)(2,1)}, bf16[2,2,4,512,256]{4,3,2,1,0:T(8,128)(2,1)}, u32[]{:S(2)}, u32[]{:S(2)}) collective-permute-start(bf16[2,2,4,512,256]{4,3,2,1,0:T(8,128)(2,1)} %bitcast.4.own_ref), channel_id=1, source_target_pairs={{0,1},{1,0},{2,3},{3,2},{4,5},{5,4},{6,7},{7,6},{8,9},{9,8},{10,11... | collective-permute-start | bytes 12582920 | tf_op jit(solution)/shard_map/ppermute | solution.py:148
  82.1 0.0 copy-done.4
  82.1 0.6 fusion.2
  84.1 0.0 copy-done.5
  84.1 0.1 compare_select_fusion
  84.2 2.7 %collective-permute-start.2 = (f32[2,128]{1,0:T(2,128)S(1)}, f32[2,128]{1,0:T(2,128)S(1)}, u32[]{:S(2)}, u32[]{:S(2)}) collective-permute-start(f32[2,128]{1,0:T(2,128)S(1)} %compare_select_fusion), channel_id=1, source_target_pairs={{0,256},{256,0},{1,257},{257,1},{2,258},{258,2},{3,259},{259,3},{4... | collective-permute-start | bytes 3080 | tf_op jit(solution)/shard_map/ppermute | solution.py:155
  86.9 0.0 copy-done.3
  86.9 0.1 copy.20
  87.1 0.1 copy.21
  87.2 0.1 compare_select_fusion.2
  87.3 0.1 pad_maximum_fusion.out_ref
  87.4 0.0 copy-done.2
  87.4 0.5 copy.17.in_ref
  87.9 2.2 %collective-permute-done.2 = f32[2,128]{1,0:T(2,128)S(1)} collective-permute-done((f32[2,128]{1,0:T(2,128)S(1)}, f32[2,128]{1,0:T(2,128)S(1)}, u32[]{:S(2)}, u32[]{:S(2)}) %collective-permute-start.2) | collective-permute-done | bytes 1056 | tf_op jit(solution)/shard_map/ppermute | solution.py:155
  90.0 0.0 collective-permute-done.1.other_ref
  90.1 7.4 %shard_map.104 = (bf16[2,2,512,2048]{3,2,1,0:T(8,128)(2,1)S(1)}, f32[512,64]{1,0:T(8,128)S(1)}) custom-call(s32[3]{0:T(128)S(1)} %pad_add_fusion.place, bf16[2,2,4,512,256]{4,3,2,1,0:T(8,128)(2,1)} %bitcast.4.own_ref, bf16[2,2,4,512,256]{4,3,2,1,0:T(8,128)(2,1)} %collective-permute-done.1.other_ref, bf16[4096,64]{1,0:T(8,128)(2,1)S(1)} %copy.17.in_ref), custom_call_target="tpu_custom_call" | custom-call | flops 268435456 | bytes 17825792 | tf_op jit(solution)/shard_map/pallas_call | solution.py:70
  97.5 0.0 copy-start.1
  97.5 3.2 %copy-done.1 = bf16[2,2,512,2048]{3,2,1,0:T(8,128)(2,1)} copy-done((bf16[2,2,512,2048]{3,2,1,0:T(8,128)(2,1)}, bf16[2,2,512,2048]{3,2,1,0:T(8,128)(2,1)S(1)}, u32[]{:S(2)}) %copy-start.1) | copy-done | bytes 8388632
  100.7 7.6 %all-gather.2.cloned.1.call-done = bf16[16,2,128,768]{3,2,1,0:T(8,128)(2,1)} async-done(((bf16[1,2,128,768]{3,2,1,0:T(8,128)(2,1)}), bf16[16,2,128,768]{3,2,1,0:T(8,128)(2,1)}) %all-gather.2.cloned.1.call-update) | async-done | bytes 6291472 | tf_op jit(solution)/shard_map/all_gather | solution.py:144
  108.3 0.1 broadcast_in_dim.28.scale_ref
  108.4 7.8 %shard_map.105 = bf16[2,32,128]{2,1,0:T(8,128)(2,1)S(1)} custom-call(bf16[2,2,512,2048]{3,2,1,0:T(8,128)(2,1)} %copy-done.1, bf16[4096,768]{1,0:T(8,128)(2,1)} %bitcast.18, f32[512,64]{1,0:T(8,128)S(1)} %get-tuple-element.12.infac_ref, f32[512,128]{1,0:T(8,128)S(1)} %broadcast_in_dim.28.scale_ref, bf16[256,128]{1,0:T(8,128)(2,1)S(1)} %pad_maximum_fusion.out_ref), custom_call_target="tpu_custom_call" | custom-call | flops 3221225472 | bytes 15728640 | tf_op jit(solution)/shard_map/pallas_call | solution.py:116
  116.3 17.9 %all_to_all.11 = bf16[32,32,128]{2,1,0:T(8,128)(2,1)S(1)} all-to-all(bf16[32,32,128]{2,1,0:T(8,128)(2,1)S(1)} %bitcast.19), channel_id=1, replica_groups=mesh['xh'=2,'z'=16,'y'=4,'xl'=2,'c'=2] {'xh','y','xl','c'}, dimensions={0} | all-to-all | bytes 524288 | tf_op jit(solution)/shard_map/all_to_all | solution.py:165
  134.2 0.1 reduce_sum.12
  134.3 0.0 copy-done
  134.3 0.8 fusion.3
  (6 shorter events, 0.1 us)
Async XLA Ops:
  6.5 127.7 %copy-start = (bf16[64,4096]{1,0:T(8,128)(2,1)S(1)}, bf16[64,4096]{1,0:T(8,128)(2,1)}, u32[]{:S(2)}) copy-start(bf16[64,4096]{1,0:T(8,128)(2,1)} %param.19) | copy-start | bytes 1572868
  6.5 101.7 %all-gather.2.cloned.1.call-start = ((), (), s32[]{:S(2)}) async-start(), calls=%async_computation.2 | async-start | bytes 6684672 | tf_op jit(solution)/shard_map/all_gather | solution.py:144
  7.8 8.5 %collective-permute-start = (bf16[128,768]{1,0:T(8,128)(2,1)S(1)}, bf16[128,768]{1,0:T(8,128)(2,1)S(1)}, u32[]{:S(2)}, u32[]{:S(2)}) collective-permute-start(bf16[128,768]{1,0:T(8,128)(2,1)S(1)} %get-tuple-element.9), channel_id=1, source_target_pairs={{0,256},{256,0},{1,257},{257,1},{2,258},{258,2},{3,259},{259,3},{4... | collective-permute-start | bytes 589832 | tf_op jit(solution)/shard_map/ppermute | solution.py:142
  19.8 62.4 %copy-start.4 = (f32[1,2]{1,0:T(1,128)S(1)}, f32[1,2]{1,0:T(1,128)}, u32[]{:S(2)}) copy-start(f32[1,2]{1,0:T(1,128)} %param.12) | copy-start | bytes 28
  19.8 64.3 %copy-start.5 = (s32[1,2]{1,0:T(1,128)S(1)}, s32[1,2]{1,0:T(1,128)}, u32[]{:S(2)}) copy-start(s32[1,2]{1,0:T(1,128)} %param.13) | copy-start | bytes 28
  19.8 67.1 %copy-start.3 = (bf16[512,64]{0,1:T(8,128)(2,1)S(1)}, bf16[512,64]{0,1:T(8,128)(2,1)}, u32[]{:S(2)}) copy-start(bf16[512,64]{0,1:T(8,128)(2,1)} %param.18) | copy-start | bytes 196612
  19.8 67.6 %copy-start.2 = (bf16[4096,64]{0,1:T(8,128)(2,1)S(1)}, bf16[4096,64]{0,1:T(8,128)(2,1)}, u32[]{:S(2)}) copy-start(bf16[4096,64]{0,1:T(8,128)(2,1)} %param.17) | copy-start | bytes 1572868
  76.7 13.4 %collective-permute-start.1 = (bf16[2,2,4,512,256]{4,3,2,1,0:T(8,128)(2,1)}, bf16[2,2,4,512,256]{4,3,2,1,0:T(8,128)(2,1)}, u32[]{:S(2)}, u32[]{:S(2)}) collective-permute-start(bf16[2,2,4,512,256]{4,3,2,1,0:T(8,128)(2,1)} %bitcast.4.own_ref), channel_id=1, source_target_pairs={{0,1},{1,0},{2,3},{3,2},{4,5},{5,4},{6,7},{7,6},{8,9},{9,8},{10,11... | collective-permute-start | bytes 12582920 | tf_op jit(solution)/shard_map/ppermute | solution.py:148
  84.2 5.9 %collective-permute-start.2 = (f32[2,128]{1,0:T(2,128)S(1)}, f32[2,128]{1,0:T(2,128)S(1)}, u32[]{:S(2)}, u32[]{:S(2)}) collective-permute-start(f32[2,128]{1,0:T(2,128)S(1)} %compare_select_fusion), channel_id=1, source_target_pairs={{0,256},{256,0},{1,257},{257,1},{2,258},{258,2},{3,259},{259,3},{4... | collective-permute-start | bytes 3080 | tf_op jit(solution)/shard_map/ppermute | solution.py:155
  97.5 3.2 %copy-start.1 = (bf16[2,2,512,2048]{3,2,1,0:T(8,128)(2,1)}, bf16[2,2,512,2048]{3,2,1,0:T(8,128)(2,1)S(1)}, u32[]{:S(2)}) copy-start(bf16[2,2,512,2048]{3,2,1,0:T(8,128)(2,1)S(1)} %get-tuple-element.10.rows_ref) | copy-start | bytes 25165828
Sparse Core Ops, SparseCore 0:
  17.3 90.9 all-gather.1

commit v3 on v2

v3 whole, which is shorter than its diff:
```python
import jax
import jax.numpy as jnp
from jax import lax
from jax.experimental import pallas as pl
from jax.experimental.pallas import tpu as pltpu
from jax.sharding import Mesh
from jax.sharding import PartitionSpec as P

SIZES = (2, 16, 4, 2, 2)
NAMES = ("xh", "z", "y", "xl", "c")
DP = ("xh", "z")
TEST = ("y", "xl", "c")
PLANE = ("xh", "y", "xl")
F32 = jnp.float32
BF16 = jnp.bfloat16
MIB = 1024 * 1024
PARTS = 8


def pack(gives, place, gate_weight, up_weight, down_weight):
    def kernel(place, gate_ref, up_ref, down_ref, packed_ref):
        xh = place[0]
        units = pl.ds(pl.multiple_of((1 - xh if gives else xh) * 256, 256), 256)
        slot = packed_ref if gives else packed_ref.at[xh]
        slot[:, :256] = gate_ref[:, units]
        slot[:, 256:512] = up_ref[:, units]
        slot[:, 512:] = down_ref[units, :].T

    here = pl.BlockSpec(memory_space=pltpu.VMEM)
    return pl.pallas_call(
        kernel,
        in_specs=[pl.BlockSpec(memory_space=pltpu.SMEM), here, here, here],
        out_specs=here,
        out_shape=jax.ShapeDtypeStruct((128, 768) if gives else (2, 128, 768), BF16),
        compiler_params=pltpu.CompilerParams(vmem_limit_bytes=8 * MIB),
        cost_estimate=pl.CostEstimate(flops=0, bytes_accessed=768 * 1024, transcendentals=0),
    )(place, *(pltpu.with_memory_space_constraint(each, pltpu.HBM) for each in (gate_weight, up_weight, down_weight)))


def order_kernel(place, own_ref, other_ref, in_ref, rows_ref, infac_ref):
    core = place[2]
    infac = jnp.zeros((512, 64), F32)
    for plane in range(16):
        ours = (plane // 2) % 2 == core
        lanes = slice(plane % 2 * 128, plane % 2 * 128 + 128)
        for half in range(2):
            into = slice(plane % 2 * 256 + half * 128, plane % 2 * 256 + half * 128 + 128)
            for pair in range(2):
                for kind in range(2):
                    slots = slice(kind * 256, kind * 256 + 256)
                    rows_ref[plane // 2, kind, pair * 256 : pair * 256 + 256, into] = jnp.where(
                        ours,
                        own_ref[pair, half, plane // 4, slots, lanes],
                        other_ref[pair, half, plane // 4, slots, lanes],
                    )
        in_rows = jnp.concatenate(
            [in_ref[(half * 16 + plane) * 128 : (half * 16 + plane) * 128 + 128, :] for half in range(2)], axis=0
        )
        infac += jnp.dot(
            rows_ref[plane // 2, 0, :, plane % 2 * 256 : plane % 2 * 256 + 256], in_rows, preferred_element_type=F32
        )
    row = lax.broadcasted_iota(jnp.int32, (64, 64), 0)
    column = lax.broadcasted_iota(jnp.int32, (64, 64), 1)
    even_first = (row == jnp.where(column < 32, 2 * column, 2 * column - 63)).astype(F32)
    infac_ref[...] = jnp.dot(infac, even_first, precision=lax.Precision.HIGHEST, preferred_element_type=F32)


def order(place, own, other, in_proj):
    here = pl.BlockSpec(memory_space=pltpu.VMEM)
    return pl.pallas_call(
        order_kernel,
        in_specs=[pl.BlockSpec(memory_space=pltpu.SMEM), here, here, here],
        out_specs=[here, here],
        out_shape=[jax.ShapeDtypeStruct((PARTS, 2, 512, 512), BF16), jax.ShapeDtypeStruct((512, 64), F32)],
        compiler_params=pltpu.CompilerParams(vmem_limit_bytes=24 * MIB),
        cost_estimate=pl.CostEstimate(flops=2 * 512 * 4096 * 64, bytes_accessed=17 * MIB, transcendentals=0),
    )(place, own, other, in_proj)


def layer_kernel(rows_ref, weight_ref, infac_ref, scale_ref, out_ref, pair_ref, rows, weights, pre, back, sems):
    copies = [
        (
            pltpu.make_async_copy(weight_ref.at[pl.ds(part * 512, 512), :], weights.at[part], sems.at[0, part]),
            pltpu.make_async_copy(rows_ref.at[part], rows.at[part], sems.at[1, part]),
        )
        for part in range(PARTS)
    ]
    for two in copies:
        for copy in two:
            copy.start()
    for part in range(PARTS):
        for copy in copies[part]:
            copy.wait()
        one = jnp.dot(rows[part, 0], weights[part, :, :512], preferred_element_type=F32)
        two = jnp.dot(rows[part, 1], weights[part, :, 512:], preferred_element_type=F32)
        if part:
            pre[...] += one
            back[...] += two
        else:
            pre[...] = one
            back[...] = two
    gate = pre[:, :256]
    sig = jax.nn.sigmoid(gate)
    slope = sig * (1.0 + gate * (1.0 - sig))
    grad = (scale_ref[:, :1] * back[...] * pre[:, 256:] * slope).astype(BF16)
    out = jnp.dot(grad, out_ref[...], preferred_element_type=F32)
    lane = lax.broadcasted_iota(jnp.int32, (32, 128), 1)
    for pair in range(2):
        slots = slice(pair * 256, pair * 256 + 256)
        mat = lax.dot_general(
            infac_ref[slots, :], out[slots, :], (((0,), (0,)), ((), ())),
            precision=lax.Precision.HIGHEST, preferred_element_type=F32,
        )
        pair_ref[pair] = jnp.where(lane < 64, mat[:32], mat[32:64]).astype(BF16)


def layer(rows, weights, infac, scale, out_twice):
    here = pl.BlockSpec(memory_space=pltpu.VMEM)
    there = pl.BlockSpec(memory_space=pl.ANY)
    rows = pltpu.with_memory_space_constraint(rows, pltpu.HBM)
    weights = pltpu.with_memory_space_constraint(weights, pltpu.HBM)
    return pl.pallas_call(
        layer_kernel,
        in_specs=[there, there, here, here, here],
        out_specs=here,
        out_shape=jax.ShapeDtypeStruct((2, 32, 128), BF16),
        scratch_shapes=[
            pltpu.VMEM((PARTS, 2, 512, 512), BF16),
            pltpu.VMEM((PARTS, 512, 768), BF16),
            pltpu.VMEM((512, 512), F32),
            pltpu.VMEM((512, 256), F32),
            pltpu.SemaphoreType.DMA((2, PARTS)),
        ],
        compiler_params=pltpu.CompilerParams(vmem_limit_bytes=40 * MIB),
        cost_estimate=pl.CostEstimate(flops=2 * 512 * 4096 * 768, bytes_accessed=15 * MIB, transcendentals=131072),
    )(rows, weights, infac, scale, out_twice)


def per_device(
    tokens, upstream, rewards, lengths, gate_weight, up_weight, down_weight, in_proj, out_proj, test_grads
):
    xh, z, core = lax.axis_index("xh"), lax.axis_index("z"), lax.axis_index("c")
    place = jnp.stack([xh, z, core]).astype(jnp.int32)
    swap = [(0, 1), (1, 0)]

    theirs = lax.ppermute(pack(True, place, gate_weight, up_weight, down_weight), "xh", swap)
    mine = pack(False, place, gate_weight, up_weight, down_weight)
    block = lax.dynamic_update_slice(mine, theirs[None], (1 - xh, 0, 0))
    weights = lax.all_gather(block, "z").reshape(4096, 768)

    acts = jnp.concatenate([tokens, upstream], axis=0) + theirs[0, 0] * 0
    own = lax.all_to_all(jnp.broadcast_to(acts[None], (16, 512, 256)), PLANE, 0, 0).reshape(2, 2, 4, 512, 256)
    other = lax.ppermute(own, "c", swap)

    position = lax.broadcasted_iota(jnp.int32, (2, 128), 1)
    side = lax.broadcasted_iota(jnp.int32, (2, 128), 0)
    coef = jax.nn.sigmoid(rewards[0, 1] - rewards[0, 0])
    live = (position < lengths.reshape(2, 1)).astype(F32)
    scale = (coef * jnp.where(side == 1, 1.0, -1.0).astype(F32) * live).reshape(2, 128)
    scale_other = lax.ppermute(scale, "xh", swap)
    scale = jnp.where(xh == 0, jnp.stack([scale, scale_other]), jnp.stack([scale_other, scale]))
    scale = jnp.broadcast_to(scale.reshape(512, 1), (512, 128))

    out_half = jnp.where(xh == 0, out_proj[:256], out_proj[256:])
    out_twice = jnp.concatenate([out_half, out_half], axis=1)

    rows, infac = order(place, own, other, in_proj)
    pairs = layer(rows, weights, infac, scale, out_twice)
    spread = jnp.broadcast_to(pairs[:, None], (2, 16, 32, 128)).reshape(32, 32, 128)
    parts = lax.all_to_all(spread, ("xh",) + TEST, 0, 0)
    flat = jnp.sum(parts.astype(F32), axis=0).astype(BF16).reshape(1, 4096)
    return lax.dot_general(flat, test_grads, (((1,), (1,)), ((), ())), preferred_element_type=F32)


def solution(mesh):
    fine = Mesh(mesh.devices.reshape(SIZES), NAMES)
    placed = (
        P(DP, TEST),
        P(DP, TEST),
        P(DP, None),
        P(DP, None),
        P(DP, TEST),
        P(DP, TEST),
        P(TEST, DP),
        P(),
        P(TEST, None),
        P(TEST, None),
    )
    return jax.shard_map(per_device, mesh=fine, in_specs=placed, out_specs=P(DP, TEST), check_vma=False)
```

time: 142 us -> 142 us (level)
    unnamed x15 -> x17, local copies, waits for them, and re-layouts: 3.96 us -> 4.71 us
    pallas_call x2 -> x3, Pallas kernels: 9.03 us -> 9.52 us  [the longest x1 7.24 us: layer(): pl.pallas_call(layer_kernel, in_specs=[there, there, here, here, here], o...]
  transfers between devices with their start and end apart: 4 -> 4, of which waited for: 3 -> 3; matrix products, arithmetic and copies ran while one was open for 2% -> 3% of each run, Pallas kernels for 5% -> 6%
where the time goes in v3:
time: 142 us; the launch traced here: 141 us
  blocking collectives  75 us (53%)
  Pallas kernels  16.6 us (12%)
  between operations  15.7 us (11%)
  starting transfers between devices  13.7 us (10%)
  waiting for transfers between devices  11.7 us (8%)
  local copies, waits for them, and re-layouts  6.48 us (5%)
    all_to_all x1, blocking collectives, per_device(): lax.all_to_all(jnp.broadcast_to(acts[None], (16, 512, 256)), PLANE, 0, 0)  56.8 us
    all_to_all x1, blocking collectives, per_device(): parts = lax.all_to_all(spread, ('xh',) + TEST, 0, 0)  18.2 us
    all_gather x1, waiting for transfers between devices, per_device(): weights = lax.all_gather(block, 'z').reshape(4096, 768)  7.63 us
    pallas_call x1, Pallas kernels, layer(): pl.pallas_call(layer_kernel, in_specs=[there, there, here, here, here], o...  7.24 us
    pallas_call x1, Pallas kernels, order(): pl.pallas_call(order_kernel, in_specs=[pl.BlockSpec(memory_space=pltpu.SM...  7.08 us
    ppermute x1, starting transfers between devices, per_device(): lax.ppermute(pack(True, place, gate_weight, up_weight, down_weight), 'xh'...  5.48 us
    ppermute x1, starting transfers between devices, per_device(): other = lax.ppermute(own, 'c', swap)  5.48 us
    unnamed x17, local copies, waits for them, and re-layouts  4.71 us
  transfers between devices with their start and end apart: 4, of which 3 were waited for; matrix products, arithmetic and copies ran while one was open for 3% of the time, Pallas kernels for 6%

profile of v3, /device:TPU:1, one launch (start us, length us, event | category | flops | bytes accessed | tf_op | source)
XLA Modules:
  0.0 141.4 jit_solution(10845686209626919612)
XLA Ops:
  6.5 0.0 copy-start
  6.5 0.0 all-gather.2.cloned.1.call-start
  6.5 0.1 pad_add_fusion.place
  6.6 1.2 shard_map.103
  7.8 5.5 %collective-permute-start = (bf16[128,768]{1,0:T(8,128)(2,1)S(1)}, bf16[128,768]{1,0:T(8,128)(2,1)S(1)}, u32[]{:S(2)}, u32[]{:S(2)}) collective-permute-start(bf16[128,768]{1,0:T(8,128)(2,1)S(1)} %shard_map.103), channel_id=1, source_target_pairs={{0,256},{256,0},{1,257},{257,1},{2,258},{258,2},{3,259},{259,3},{4... | collective-permute-start | bytes 589832 | tf_op jit(solution)/shard_map/ppermute | solution.py:146
  13.3 1.1 shard_map.105
  14.4 1.9 %collective-permute-done = bf16[128,768]{1,0:T(8,128)(2,1)S(1)} collective-permute-done((bf16[128,768]{1,0:T(8,128)(2,1)S(1)}, bf16[128,768]{1,0:T(8,128)(2,1)S(1)}, u32[]{:S(2)}, u32[]{:S(2)}) %collective-permute-start) | collective-permute-done | bytes 196640 | tf_op jit(solution)/shard_map/ppermute | solution.py:146
  16.3 0.0 copy-start.2
  16.3 0.7 copy-done.2
  17.1 0.0 all-gather.2.cloned.1.call-update
  17.1 0.5 slice.20
  18.3 1.0 maximum_add_fusion
  19.3 0.4 broadcast_in_dim.14
  19.7 0.0 copy-start.5
  19.7 0.0 copy-start.6
  19.7 0.0 copy-start.4
  19.8 0.0 copy-start.3
  19.8 56.8 %all_to_all.10 = bf16[16,512,256]{2,1,0:T(8,128)(2,1)} all-to-all(bf16[16,512,256]{2,1,0:T(8,128)(2,1)S(1)} %broadcast_in_dim.14), channel_id=1, replica_groups=mesh['xh'=2,'z'=16,'y'=4,'xl'=2,'c'=2] {'xh','y','xl'}, dimensions={0} | all-to-all | bytes 8388608 | tf_op jit(solution)/shard_map/all_to_all | solution.py:152
  76.6 5.5 %collective-permute-start.1 = (bf16[2,2,4,512,256]{4,3,2,1,0:T(8,128)(2,1)}, bf16[2,2,4,512,256]{4,3,2,1,0:T(8,128)(2,1)}, u32[]{:S(2)}, u32[]{:S(2)}) collective-permute-start(bf16[2,2,4,512,256]{4,3,2,1,0:T(8,128)(2,1)} %bitcast.4.own_ref), channel_id=1, source_target_pairs={{0,1},{1,0},{2,3},{3,2},{4,5},{5,4},{6,7},{7,6},{8,9},{9,8},{10,11... | collective-permute-start | bytes 12582920 | tf_op jit(solution)/shard_map/ppermute | solution.py:153
  82.1 0.0 copy-done.5
  82.1 0.7 fusion.2
  84.2 0.0 copy-done.6
  84.2 0.1 compare_select_fusion
  84.3 2.7 %collective-permute-start.2 = (f32[2,128]{1,0:T(2,128)S(1)}, f32[2,128]{1,0:T(2,128)S(1)}, u32[]{:S(2)}, u32[]{:S(2)}) collective-permute-start(f32[2,128]{1,0:T(2,128)S(1)} %compare_select_fusion), channel_id=1, source_target_pairs={{0,256},{256,0},{1,257},{257,1},{2,258},{258,2},{3,259},{259,3},{4... | collective-permute-start | bytes 3080 | tf_op jit(solution)/shard_map/ppermute | solution.py:160
  87.0 0.0 copy-done.4
  87.1 0.1 copy.20
  87.2 0.1 copy.21
  87.3 0.1 compare_select_fusion.2
  87.4 0.1 pad_maximum_fusion.out_ref
  87.5 0.0 copy-done.3
  87.5 0.5 copy.17.in_ref
  88.0 2.2 %collective-permute-done.2 = f32[2,128]{1,0:T(2,128)S(1)} collective-permute-done((f32[2,128]{1,0:T(2,128)S(1)}, f32[2,128]{1,0:T(2,128)S(1)}, u32[]{:S(2)}, u32[]{:S(2)}) %collective-permute-start.2) | collective-permute-done | bytes 1056 | tf_op jit(solution)/shard_map/ppermute | solution.py:160
  90.2 0.0 collective-permute-done.1.other_ref
  90.2 7.1 %shard_map.104 = (bf16[8,2,512,512]{3,2,1,0:T(8,128)(2,1)S(1)}, f32[512,64]{1,0:T(8,128)S(1)}) custom-call(s32[3]{0:T(128)S(1)} %pad_add_fusion.place, bf16[2,2,4,512,256]{4,3,2,1,0:T(8,128)(2,1)} %bitcast.4.own_ref, bf16[2,2,4,512,256]{4,3,2,1,0:T(8,128)(2,1)} %collective-permute-done.1.other_ref, bf16[4096,64]{1,0:T(8,128)(2,1)S(1)} %copy.17.in_ref), custom_call_target="tpu_custom_call" | custom-call | flops 268435456 | bytes 17825792 | tf_op jit(solution)/shard_map/pallas_call | solution.py:70
  97.3 0.0 copy-start.1
  97.3 3.2 %copy-done.1 = bf16[8,2,512,512]{3,2,1,0:T(8,128)(2,1)} copy-done((bf16[8,2,512,512]{3,2,1,0:T(8,128)(2,1)}, bf16[8,2,512,512]{3,2,1,0:T(8,128)(2,1)S(1)}, u32[]{:S(2)}) %copy-start.1) | copy-done | bytes 8388632
  100.5 7.6 %all-gather.2.cloned.1.call-done = bf16[16,2,128,768]{3,2,1,0:T(8,128)(2,1)} async-done(((bf16[1,2,128,768]{3,2,1,0:T(8,128)(2,1)}), bf16[16,2,128,768]{3,2,1,0:T(8,128)(2,1)}) %all-gather.2.cloned.1.call-update) | async-done | bytes 6291472 | tf_op jit(solution)/shard_map/all_gather | solution.py:149
  108.1 0.1 broadcast_in_dim.29.scale_ref
  108.2 7.2 %shard_map.106 = bf16[2,32,128]{2,1,0:T(8,128)(2,1)S(1)} custom-call(bf16[8,2,512,512]{3,2,1,0:T(8,128)(2,1)} %copy-done.1, bf16[4096,768]{1,0:T(8,128)(2,1)} %bitcast.19, f32[512,64]{1,0:T(8,128)S(1)} %get-tuple-element.8.infac_ref, f32[512,128]{1,0:T(8,128)S(1)} %broadcast_in_dim.29.scale_ref, bf16[256,128]{1,0:T(8,128)(2,1)S(1)} %pad_maximum_fusion.out_ref), custom_call_target="tpu_custom_call" | custom-call | flops 3221225472 | bytes 15728640 | tf_op jit(solution)/shard_map/pallas_call | solution.py:122
  115.5 18.2 %all_to_all.11 = bf16[32,32,128]{2,1,0:T(8,128)(2,1)S(1)} all-to-all(bf16[32,32,128]{2,1,0:T(8,128)(2,1)S(1)} %bitcast.20), channel_id=1, replica_groups=mesh['xh'=2,'z'=16,'y'=4,'xl'=2,'c'=2] {'xh','y','xl','c'}, dimensions={0} | all-to-all | bytes 524288 | tf_op jit(solution)/shard_map/all_to_all | solution.py:170
  133.7 0.1 reduce_sum.12
  133.8 0.0 copy-done
  133.8 0.8 fusion.3
  (7 shorter events, 0.1 us)
Async XLA Ops:
  6.5 127.2 %copy-start = (bf16[64,4096]{1,0:T(8,128)(2,1)S(1)}, bf16[64,4096]{1,0:T(8,128)(2,1)}, u32[]{:S(2)}) copy-start(bf16[64,4096]{1,0:T(8,128)(2,1)} %param.19) | copy-start | bytes 1572868
  6.5 101.6 %all-gather.2.cloned.1.call-start = ((), (), s32[]{:S(2)}) async-start(), calls=%async_computation.2 | async-start | bytes 6684672 | tf_op jit(solution)/shard_map/all_gather | solution.py:149
  7.8 8.5 %collective-permute-start = (bf16[128,768]{1,0:T(8,128)(2,1)S(1)}, bf16[128,768]{1,0:T(8,128)(2,1)S(1)}, u32[]{:S(2)}, u32[]{:S(2)}) collective-permute-start(bf16[128,768]{1,0:T(8,128)(2,1)S(1)} %shard_map.103), channel_id=1, source_target_pairs={{0,256},{256,0},{1,257},{257,1},{2,258},{258,2},{3,259},{259,3},{4... | collective-permute-start | bytes 589832 | tf_op jit(solution)/shard_map/ppermute | solution.py:146
  16.3 0.8 copy-start.2
  19.7 62.4 %copy-start.5 = (f32[1,2]{1,0:T(1,128)S(1)}, f32[1,2]{1,0:T(1,128)}, u32[]{:S(2)}) copy-start(f32[1,2]{1,0:T(1,128)} %param.12) | copy-start | bytes 28
  19.7 64.5 %copy-start.6 = (s32[1,2]{1,0:T(1,128)S(1)}, s32[1,2]{1,0:T(1,128)}, u32[]{:S(2)}) copy-start(s32[1,2]{1,0:T(1,128)} %param.13) | copy-start | bytes 28
  19.7 67.3 %copy-start.4 = (bf16[512,64]{0,1:T(8,128)(2,1)S(1)}, bf16[512,64]{0,1:T(8,128)(2,1)}, u32[]{:S(2)}) copy-start(bf16[512,64]{0,1:T(8,128)(2,1)} %param.18) | copy-start | bytes 196612
  19.8 67.7 %copy-start.3 = (bf16[4096,64]{0,1:T(8,128)(2,1)S(1)}, bf16[4096,64]{0,1:T(8,128)(2,1)}, u32[]{:S(2)}) copy-start(bf16[4096,64]{0,1:T(8,128)(2,1)} %param.17) | copy-start | bytes 1572868
  76.6 13.6 %collective-permute-start.1 = (bf16[2,2,4,512,256]{4,3,2,1,0:T(8,128)(2,1)}, bf16[2,2,4,512,256]{4,3,2,1,0:T(8,128)(2,1)}, u32[]{:S(2)}, u32[]{:S(2)}) collective-permute-start(bf16[2,2,4,512,256]{4,3,2,1,0:T(8,128)(2,1)} %bitcast.4.own_ref), channel_id=1, source_target_pairs={{0,1},{1,0},{2,3},{3,2},{4,5},{5,4},{6,7},{7,6},{8,9},{9,8},{10,11... | collective-permute-start | bytes 12582920 | tf_op jit(solution)/shard_map/ppermute | solution.py:153
  84.3 5.9 %collective-permute-start.2 = (f32[2,128]{1,0:T(2,128)S(1)}, f32[2,128]{1,0:T(2,128)S(1)}, u32[]{:S(2)}, u32[]{:S(2)}) collective-permute-start(f32[2,128]{1,0:T(2,128)S(1)} %compare_select_fusion), channel_id=1, source_target_pairs={{0,256},{256,0},{1,257},{257,1},{2,258},{258,2},{3,259},{259,3},{4... | collective-permute-start | bytes 3080 | tf_op jit(solution)/shard_map/ppermute | solution.py:160
  97.3 3.2 %copy-start.1 = (bf16[8,2,512,512]{3,2,1,0:T(8,128)(2,1)}, bf16[8,2,512,512]{3,2,1,0:T(8,128)(2,1)S(1)}, u32[]{:S(2)}) copy-start(bf16[8,2,512,512]{3,2,1,0:T(8,128)(2,1)S(1)} %get-tuple-element.7.rows_ref) | copy-start | bytes 25165828
Sparse Core Ops, SparseCore 0:
  17.2 90.8 all-gather.1

commit v4 on v3

v4 whole, which is shorter than its diff:
```python
import jax
import jax.numpy as jnp
from jax import lax
from jax.experimental import pallas as pl
from jax.experimental.pallas import tpu as pltpu
from jax.sharding import Mesh
from jax.sharding import PartitionSpec as P

SIZES = (2, 16, 4, 2, 2)
NAMES = ("xh", "z", "y", "xl", "c")
DP = ("xh", "z")
TEST = ("y", "xl", "c")
PLANE = ("xh", "y", "xl")
F32 = jnp.float32
BF16 = jnp.bfloat16
MIB = 1024 * 1024
PARTS = 8


def pack(gives, place, gate_weight, up_weight, down_weight):
    def kernel(place, gate_ref, up_ref, down_ref, packed_ref):
        xh = place[0]
        units = pl.ds(pl.multiple_of((1 - xh if gives else xh) * 256, 256), 256)
        slot = packed_ref if gives else packed_ref.at[xh]
        slot[:, :256] = gate_ref[:, units]
        slot[:, 256:512] = up_ref[:, units]
        slot[:, 512:] = down_ref[units, :].T

    here = pl.BlockSpec(memory_space=pltpu.VMEM)
    return pl.pallas_call(
        kernel,
        in_specs=[pl.BlockSpec(memory_space=pltpu.SMEM), here, here, here],
        out_specs=here,
        out_shape=jax.ShapeDtypeStruct((128, 768) if gives else (2, 128, 768), BF16),
        compiler_params=pltpu.CompilerParams(vmem_limit_bytes=8 * MIB),
        cost_estimate=pl.CostEstimate(flops=0, bytes_accessed=768 * 1024, transcendentals=0),
    )(place, *(pltpu.with_memory_space_constraint(each, pltpu.HBM) for each in (gate_weight, up_weight, down_weight)))


def live_blocks(place):
    counts = [(place[3 + n] + 15) // 16 for n in range(4)]
    starts = [jnp.int32(0)]
    for count in counts:
        starts.append(starts[-1] + count)
    return counts, starts


def order_kernel(place, own_ref, other_ref, in_ref, scale_ref, rows_ref, infac_ref, packed_ref):
    core = place[2]
    counts, starts = live_blocks(place)
    for sequence in range(4):
        pair, side = sequence // 2, sequence % 2

        def move(n, carry):
            source = pl.multiple_of(side * 128 + n * 16, 16)
            target = pl.ds(pl.multiple_of((starts[sequence] + n) * 16, 16), 16)
            for plane in range(16):
                ours = (plane // 2) % 2 == core
                lanes = slice(plane % 2 * 128, plane % 2 * 128 + 128)
                for half in range(2):
                    into = slice(plane % 2 * 256 + half * 128, plane % 2 * 256 + half * 128 + 128)
                    for kind in range(2):
                        slots = pl.ds(pl.multiple_of(kind * 256 + source, 16), 16)
                        rows_ref[plane // 2, kind, target, into] = jnp.where(
                            ours,
                            own_ref[pair, half, plane // 4, slots, lanes],
                            other_ref[pair, half, plane // 4, slots, lanes],
                        )
            packed_ref[target, :] = scale_ref[pl.ds(pl.multiple_of(pair * 256 + source, 16), 16), :]
            return carry

        lax.fori_loop(0, counts[sequence], move, 0)

    def clear(n, carry):
        target = pl.ds(pl.multiple_of(n * 16, 16), 16)
        for part in range(PARTS):
            for kind in range(2):
                rows_ref[part, kind, target, :] = jnp.zeros((16, 512), BF16)
        packed_ref[target, :] = jnp.zeros((16, 128), F32)
        return carry

    lax.fori_loop(starts[4], jnp.where(starts[4] > 16, 32, 16), clear, 0)

    infac = jnp.zeros((512, 64), F32)
    for plane in range(16):
        in_rows = jnp.concatenate(
            [in_ref[(half * 16 + plane) * 128 : (half * 16 + plane) * 128 + 128, :] for half in range(2)], axis=0
        )
        infac += jnp.dot(
            rows_ref[plane // 2, 0, :, plane % 2 * 256 : plane % 2 * 256 + 256], in_rows, preferred_element_type=F32
        )
    row = lax.broadcasted_iota(jnp.int32, (64, 64), 0)
    column = lax.broadcasted_iota(jnp.int32, (64, 64), 1)
    even_first = (row == jnp.where(column < 32, 2 * column, 2 * column - 63)).astype(F32)
    infac = jnp.dot(infac, even_first, precision=lax.Precision.HIGHEST, preferred_element_type=F32)
    first = lax.broadcasted_iota(jnp.int32, (512, 64), 0) < starts[2] * 16
    infac_ref[...] = jnp.concatenate([jnp.where(first, infac, 0.0), jnp.where(first, 0.0, infac)], axis=1)


def order(place, own, other, in_proj, scale):
    here = pl.BlockSpec(memory_space=pltpu.VMEM)
    return pl.pallas_call(
        order_kernel,
        in_specs=[pl.BlockSpec(memory_space=pltpu.SMEM), here, here, here, here],
        out_specs=[here, here, here],
        out_shape=[
            jax.ShapeDtypeStruct((PARTS, 2, 512, 512), BF16),
            jax.ShapeDtypeStruct((512, 128), F32),
            jax.ShapeDtypeStruct((512, 128), F32),
        ],
        compiler_params=pltpu.CompilerParams(vmem_limit_bytes=24 * MIB),
        cost_estimate=pl.CostEstimate(flops=2 * 512 * 4096 * 64, bytes_accessed=17 * MIB, transcendentals=0),
    )(place, own, other, in_proj, scale)


def layer_kernel(
    place, rows_ref, weight_ref, infac_ref, scale_ref, out_ref, pair_ref, rows, weights, pre, back, sems
):
    def run(count):
        some = slice(0, count)
        copies = [
            (
                pltpu.make_async_copy(weight_ref.at[pl.ds(part * 512, 512), :], weights.at[part], sems.at[0, part]),
                pltpu.make_async_copy(rows_ref.at[part, :, some, :], rows.at[part, :, some, :], sems.at[1, part]),
            )
            for part in range(PARTS)
        ]
        for both in copies:
            for copy in both:
                copy.start()
        for part in range(PARTS):
            for copy in copies[part]:
                copy.wait()
            one = jnp.dot(rows[part, 0, some], weights[part, :, :512], preferred_element_type=F32)
            two = jnp.dot(rows[part, 1, some], weights[part, :, 512:], preferred_element_type=F32)
            if part:
                pre[some, :] += one
                back[some, :] += two
            else:
                pre[some, :] = one
                back[some, :] = two
        gate = pre[some, :256]
        sig = jax.nn.sigmoid(gate)
        slope = sig * (1.0 + gate * (1.0 - sig))
        grad = (scale_ref[some, :1] * back[some, :] * pre[some, 256:] * slope).astype(BF16)
        out = jnp.dot(grad, out_ref[...], preferred_element_type=F32)
        mats = lax.dot_general(
            infac_ref[some, :], out, (((0,), (0,)), ((), ())),
            precision=lax.Precision.HIGHEST, preferred_element_type=F32,
        )
        lane = lax.broadcasted_iota(jnp.int32, (32, 128), 1)
        for pair in range(2):
            mat = mats[pair * 64 : pair * 64 + 64]
            pair_ref[pair] = jnp.where(lane < 64, mat[:32], mat[32:]).astype(BF16)

    few = live_blocks(place)[1][4] <= 16
    pl.when(few)(lambda: run(256))
    pl.when(jnp.logical_not(few))(lambda: run(512))


def layer(place, rows, weights, infac, scale, out_twice):
    here = pl.BlockSpec(memory_space=pltpu.VMEM)
    there = pl.BlockSpec(memory_space=pl.ANY)
    rows = pltpu.with_memory_space_constraint(rows, pltpu.HBM)
    weights = pltpu.with_memory_space_constraint(weights, pltpu.HBM)
    return pl.pallas_call(
        layer_kernel,
        in_specs=[pl.BlockSpec(memory_space=pltpu.SMEM), there, there, here, here, here],
        out_specs=here,
        out_shape=jax.ShapeDtypeStruct((2, 32, 128), BF16),
        scratch_shapes=[
            pltpu.VMEM((PARTS, 2, 512, 512), BF16),
            pltpu.VMEM((PARTS, 512, 768), BF16),
            pltpu.VMEM((512, 512), F32),
            pltpu.VMEM((512, 256), F32),
            pltpu.SemaphoreType.DMA((2, PARTS)),
        ],
        compiler_params=pltpu.CompilerParams(vmem_limit_bytes=40 * MIB),
        cost_estimate=pl.CostEstimate(flops=2 * 512 * 4096 * 768, bytes_accessed=15 * MIB, transcendentals=131072),
    )(place, rows, weights, infac, scale, out_twice)


def per_device(
    tokens, upstream, rewards, lengths, gate_weight, up_weight, down_weight, in_proj, out_proj, test_grads
):
    xh, z, core = lax.axis_index("xh"), lax.axis_index("z"), lax.axis_index("c")
    place = jnp.stack([xh, z, core]).astype(jnp.int32)
    swap = [(0, 1), (1, 0)]

    theirs = lax.ppermute(pack(True, place, gate_weight, up_weight, down_weight), "xh", swap)
    mine = pack(False, place, gate_weight, up_weight, down_weight)
    block = lax.dynamic_update_slice(mine, theirs[None], (1 - xh, 0, 0))
    weights = lax.all_gather(block, "z").reshape(4096, 768)

    acts = jnp.concatenate([tokens, upstream], axis=0) + theirs[0, 0] * 0
    own = lax.all_to_all(jnp.broadcast_to(acts[None], (16, 512, 256)), PLANE, 0, 0).reshape(2, 2, 4, 512, 256)
    other = lax.ppermute(own, "c", swap)

    coef = jax.nn.sigmoid(rewards[0, 1] - rewards[0, 0])
    known = jnp.pad(jnp.stack([coef, lengths[0, 0].astype(F32), lengths[0, 1].astype(F32)]), (0, 125))[None]
    known_other = lax.ppermute(known, "xh", swap)
    known = jnp.where(xh == 0, jnp.concatenate([known, known_other]), jnp.concatenate([known_other, known]))
    position = lax.broadcasted_iota(jnp.int32, (2, 2, 128), 2).astype(F32)
    side = lax.broadcasted_iota(jnp.int32, (2, 2, 128), 1)
    live = (position < known[:, 1:3, None]).astype(F32)
    scale = known[:, :1, None] * jnp.where(side == 1, 1.0, -1.0).astype(F32) * live
    scale = jnp.broadcast_to(scale.reshape(512, 1), (512, 128))
    ready = jnp.concatenate([place, known[:, 1:3].reshape(4).astype(jnp.int32)])

    out_half = jnp.where(xh == 0, out_proj[:256], out_proj[256:])
    out_twice = jnp.concatenate([out_half, out_half], axis=1)

    rows, infac, packed = order(ready, own, other, in_proj, scale)
    pairs = layer(ready, rows, weights, infac, packed, out_twice)
    spread = jnp.broadcast_to(pairs[:, None], (2, 16, 32, 128)).reshape(32, 32, 128)
    parts = lax.all_to_all(spread, ("xh",) + TEST, 0, 0)
    flat = jnp.sum(parts.astype(F32), axis=0).astype(BF16).reshape(1, 4096)
    return lax.dot_general(flat, test_grads, (((1,), (1,)), ((), ())), preferred_element_type=F32)


def solution(mesh):
    fine = Mesh(mesh.devices.reshape(SIZES), NAMES)
    placed = (
        P(DP, TEST),
        P(DP, TEST),
        P(DP, None),
        P(DP, None),
        P(DP, TEST),
        P(DP, TEST),
        P(TEST, DP),
        P(),
        P(TEST, None),
        P(TEST, None),
    )
    return jax.shard_map(per_device, mesh=fine, in_specs=placed, out_specs=P(DP, TEST), check_vma=False)
```

time: 142 us -> 142 us (level)
  waiting for transfers between devices: 11.7 us -> 9.8 us
    all_gather x1, waiting for transfers between devices: 7.63 us -> 5.66 us  [per_device(): weights = lax.all_gather(block, 'z').reshape(4096, 768)]
where the time goes in v4:
time: 142 us
  blocking collectives  75.1 us (53%)
  Pallas kernels  16.9 us (12%)
  between operations  16.9 us (12%)
  starting transfers between devices  13.7 us (10%)
  waiting for transfers between devices  9.8 us (7%)
  local copies, waits for them, and re-layouts  7.2 us (5%)
  other arithmetic  1.57 us (1%)
    all_to_all x1, blocking collectives, per_device(): lax.all_to_all(jnp.broadcast_to(acts[None], (16, 512, 256)), PLANE, 0, 0)  56.8 us
    all_to_all x1, blocking collectives, per_device(): parts = lax.all_to_all(spread, ('xh',) + TEST, 0, 0)  18.2 us
    pallas_call x1, Pallas kernels, layer(): pl.pallas_call(layer_kernel, in_specs=[pl.BlockSpec(memory_space=pltpu.SM...  7.9 us
    pallas_call x1, Pallas kernels, order(): pl.pallas_call(order_kernel, in_specs=[pl.BlockSpec(memory_space=pltpu.SM...  6.75 us
    all_gather x1, waiting for transfers between devices, per_device(): weights = lax.all_gather(block, 'z').reshape(4096, 768)  5.66 us
    ppermute x1, starting transfers between devices, per_device(): other = lax.ppermute(own, 'c', swap)  5.49 us
    ppermute x1, starting transfers between devices, per_device(): lax.ppermute(pack(True, place, gate_weight, up_weight, down_weight), 'xh'...  5.48 us
    unnamed x17, local copies, waits for them, and re-layouts  4.7 us
  transfers between devices with their start and end apart: 4, of which 3 were waited for; matrix products, arithmetic and copies ran while one was open for 3% of the time, Pallas kernels for 6%

profile of v4, /device:TPU:1, one launch (start us, length us, event | category | flops | bytes accessed | tf_op | source)
XLA Modules:
  0.0 141.9 jit_solution(12312792579702167372)
XLA Ops:
  6.5 0.0 copy-start
  6.5 0.0 all-gather.2.cloned.1.call-start
  6.5 0.1 pad_add_fusion.1.place
  6.6 1.2 shard_map.100
  7.8 5.5 %collective-permute-start.1 = (bf16[128,768]{1,0:T(8,128)(2,1)S(1)}, bf16[128,768]{1,0:T(8,128)(2,1)S(1)}, u32[]{:S(2)}, u32[]{:S(2)}) collective-permute-start(bf16[128,768]{1,0:T(8,128)(2,1)S(1)} %shard_map.100), channel_id=1, source_target_pairs={{0,256},{256,0},{1,257},{257,1},{2,258},{258,2},{3,259},{259,3},{4... | collective-permute-start | bytes 589832 | tf_op jit(solution)/shard_map/ppermute | solution.py:190
  13.3 1.1 shard_map.102
  14.4 1.9 %collective-permute-done.1 = bf16[128,768]{1,0:T(8,128)(2,1)S(1)} collective-permute-done((bf16[128,768]{1,0:T(8,128)(2,1)S(1)}, bf16[128,768]{1,0:T(8,128)(2,1)S(1)}, u32[]{:S(2)}, u32[]{:S(2)}) %collective-permute-start.1) | collective-permute-done | bytes 196640 | tf_op jit(solution)/shard_map/ppermute | solution.py:190
  16.3 0.0 copy-start.2
  16.3 0.8 copy-done.2
  17.1 0.0 all-gather.2.cloned.1.call-update
  17.1 0.5 slice.37
  18.3 1.0 maximum_add_fusion
  19.3 0.4 broadcast_in_dim.17
  19.7 0.0 copy-start.5
  19.7 0.0 copy-start.6
  19.8 0.0 copy-start.4
  19.8 0.0 copy-start.3
  19.8 56.8 %all_to_all.10 = bf16[16,512,256]{2,1,0:T(8,128)(2,1)} all-to-all(bf16[16,512,256]{2,1,0:T(8,128)(2,1)S(1)} %broadcast_in_dim.17), channel_id=1, replica_groups=mesh['xh'=2,'z'=16,'y'=4,'xl'=2,'c'=2] {'xh','y','xl'}, dimensions={0} | all-to-all | bytes 8388608 | tf_op jit(solution)/shard_map/all_to_all | solution.py:196
  76.6 5.5 %collective-permute-start.2 = (bf16[2,2,4,512,256]{4,3,2,1,0:T(8,128)(2,1)}, bf16[2,2,4,512,256]{4,3,2,1,0:T(8,128)(2,1)}, u32[]{:S(2)}, u32[]{:S(2)}) collective-permute-start(bf16[2,2,4,512,256]{4,3,2,1,0:T(8,128)(2,1)} %bitcast.8.own_ref), channel_id=1, source_target_pairs={{0,1},{1,0},{2,3},{3,2},{4,5},{5,4},{6,7},{7,6},{8,9},{9,8},{10,11... | collective-permute-start | bytes 12582920 | tf_op jit(solution)/shard_map/ppermute | solution.py:197
  82.1 0.0 copy-done.5
  82.1 0.6 fusion.3
  84.0 0.0 copy-done.6
  84.0 0.6 fusion.4
  85.9 0.1 fusion
  86.0 2.7 %collective-permute-start = (f32[1,128]{1,0:T(1,128)S(1)}, f32[1,128]{1,0:T(1,128)S(1)}, u32[]{:S(2)}, u32[]{:S(2)}) collective-permute-start(f32[1,128]{1,0:T(1,128)S(1)} %fusion), channel_id=1, source_target_pairs={{0,256},{256,0},{1,257},{257,1},{2,258},{258,2},{3,259},{259,3},{4... | collective-permute-start | bytes 1544 | tf_op jit(solution)/shard_map/ppermute | solution.py:201
  88.7 0.0 copy-done.4
  88.7 0.1 copy.23
  88.9 0.1 copy.24
  89.0 0.1 pad_maximum_fusion.out_ref
  89.1 0.0 copy-done.3
  89.1 0.5 copy.20.in_ref
  89.6 2.2 %collective-permute-done = f32[1,128]{1,0:T(1,128)S(1)} collective-permute-done((f32[1,128]{1,0:T(1,128)S(1)}, f32[1,128]{1,0:T(1,128)S(1)}, u32[]{:S(2)}, u32[]{:S(2)}) %collective-permute-start) | collective-permute-done | bytes 544 | tf_op jit(solution)/shard_map/ppermute | solution.py:201
  91.8 0.1 fusion.2
  91.9 0.1 convert_element_type.26
  92.0 0.1 pad_add_fusion.place
  92.1 0.1 slice_reduce_fusion
  92.2 0.1 compare_select_fusion
  92.3 0.0 collective-permute-done.2.other_ref
  92.3 0.1 broadcast_in_dim.35.scale_ref
  92.4 6.8 %shard_map.101 = (bf16[8,2,512,512]{3,2,1,0:T(8,128)(2,1)S(1)}, f32[512,128]{1,0:T(8,128)S(1)}, f32[512,128]{1,0:T(8,128)S(1)}) custom-call(s32[7]{0:T(128)S(1)} %pad_add_fusion.place, bf16[2,2,4,512,256]{4,3,2,1,0:T(8,128)(2,1)} %bitcast.8.own_ref, bf16[2,2,4,512,256]{4,3,2,1,0:T(8,128)(2,1)} %collective-permute-done.2.other_ref, ...), custom_call_target="tpu_custom_call" | custom-call | flops 268435456 | bytes 17825792 | tf_op jit(solution)/shard_map/pallas_call | solution.py:102
  99.2 0.0 copy-start.1
  99.2 3.2 %copy-done.1 = bf16[8,2,512,512]{3,2,1,0:T(8,128)(2,1)} copy-done((bf16[8,2,512,512]{3,2,1,0:T(8,128)(2,1)}, bf16[8,2,512,512]{3,2,1,0:T(8,128)(2,1)S(1)}, u32[]{:S(2)}) %copy-start.1) | copy-done | bytes 8388632
  102.4 5.7 %all-gather.2.cloned.1.call-done = bf16[16,2,128,768]{3,2,1,0:T(8,128)(2,1)} async-done(((bf16[1,2,128,768]{3,2,1,0:T(8,128)(2,1)}), bf16[16,2,128,768]{3,2,1,0:T(8,128)(2,1)}) %all-gather.2.cloned.1.call-update) | async-done | bytes 6291472 | tf_op jit(solution)/shard_map/all_gather | solution.py:193
  108.0 7.9 %shard_map.103 = bf16[2,32,128]{2,1,0:T(8,128)(2,1)S(1)} custom-call(s32[7]{0:T(128)S(1)} %pad_add_fusion.place, bf16[8,2,512,512]{3,2,1,0:T(8,128)(2,1)} %copy-done.1, bf16[4096,768]{1,0:T(8,128)(2,1)} %bitcast.21, f32[512,128]{1,0:T(8,128)S(1)} %get-tuple-element.9.infac_ref, f32[512,128]{1,0:T(8,128)S(1)} %get-tuple-element.10.scale_ref, ...), custom_call_target="tpu_custom_call" | custom-call | flops 3221225472 | bytes 15728640 | tf_op jit(solution)/shard_map/pallas_call | solution.py:166
  116.0 18.2 %all_to_all.11 = bf16[32,32,128]{2,1,0:T(8,128)(2,1)S(1)} all-to-all(bf16[32,32,128]{2,1,0:T(8,128)(2,1)S(1)} %bitcast.22), channel_id=1, replica_groups=mesh['xh'=2,'z'=16,'y'=4,'xl'=2,'c'=2] {'xh','y','xl','c'}, dimensions={0} | all-to-all | bytes 524288 | tf_op jit(solution)/shard_map/all_to_all | solution.py:216
  134.2 0.1 reduce_sum.12
  134.3 0.0 copy-done
  134.3 0.8 fusion.5
  (8 shorter events, 0.1 us)
Async XLA Ops:
  6.5 127.8 %copy-start = (bf16[64,4096]{1,0:T(8,128)(2,1)S(1)}, bf16[64,4096]{1,0:T(8,128)(2,1)}, u32[]{:S(2)}) copy-start(bf16[64,4096]{1,0:T(8,128)(2,1)} %param.19) | copy-start | bytes 1572868
  6.5 101.5 %all-gather.2.cloned.1.call-start = ((), (), s32[]{:S(2)}) async-start(), calls=%async_computation.2 | async-start | bytes 6684672 | tf_op jit(solution)/shard_map/all_gather | solution.py:193
  7.8 8.5 %collective-permute-start.1 = (bf16[128,768]{1,0:T(8,128)(2,1)S(1)}, bf16[128,768]{1,0:T(8,128)(2,1)S(1)}, u32[]{:S(2)}, u32[]{:S(2)}) collective-permute-start(bf16[128,768]{1,0:T(8,128)(2,1)S(1)} %shard_map.100), channel_id=1, source_target_pairs={{0,256},{256,0},{1,257},{257,1},{2,258},{258,2},{3,259},{259,3},{4... | collective-permute-start | bytes 589832 | tf_op jit(solution)/shard_map/ppermute | solution.py:190
  16.3 0.8 copy-start.2
  19.7 62.4 %copy-start.5 = (f32[1,2]{1,0:T(1,128)S(1)}, f32[1,2]{1,0:T(1,128)}, u32[]{:S(2)}) copy-start(f32[1,2]{1,0:T(1,128)} %param.12) | copy-start | bytes 28
  19.7 64.2 %copy-start.6 = (s32[1,2]{1,0:T(1,128)S(1)}, s32[1,2]{1,0:T(1,128)}, u32[]{:S(2)}) copy-start(s32[1,2]{1,0:T(1,128)} %param.13) | copy-start | bytes 28
  19.8 69.0 %copy-start.4 = (bf16[512,64]{0,1:T(8,128)(2,1)S(1)}, bf16[512,64]{0,1:T(8,128)(2,1)}, u32[]{:S(2)}) copy-start(bf16[512,64]{0,1:T(8,128)(2,1)} %param.18) | copy-start | bytes 196612
  19.8 69.4 %copy-start.3 = (bf16[4096,64]{0,1:T(8,128)(2,1)S(1)}, bf16[4096,64]{0,1:T(8,128)(2,1)}, u32[]{:S(2)}) copy-start(bf16[4096,64]{0,1:T(8,128)(2,1)} %param.17) | copy-start | bytes 1572868
  76.6 15.7 %collective-permute-start.2 = (bf16[2,2,4,512,256]{4,3,2,1,0:T(8,128)(2,1)}, bf16[2,2,4,512,256]{4,3,2,1,0:T(8,128)(2,1)}, u32[]{:S(2)}, u32[]{:S(2)}) collective-permute-start(bf16[2,2,4,512,256]{4,3,2,1,0:T(8,128)(2,1)} %bitcast.8.own_ref), channel_id=1, source_target_pairs={{0,1},{1,0},{2,3},{3,2},{4,5},{5,4},{6,7},{7,6},{8,9},{9,8},{10,11... | collective-permute-start | bytes 12582920 | tf_op jit(solution)/shard_map/ppermute | solution.py:197
  86.0 5.9 %collective-permute-start = (f32[1,128]{1,0:T(1,128)S(1)}, f32[1,128]{1,0:T(1,128)S(1)}, u32[]{:S(2)}, u32[]{:S(2)}) collective-permute-start(f32[1,128]{1,0:T(1,128)S(1)} %fusion), channel_id=1, source_target_pairs={{0,256},{256,0},{1,257},{257,1},{2,258},{258,2},{3,259},{259,3},{4... | collective-permute-start | bytes 1544 | tf_op jit(solution)/shard_map/ppermute | solution.py:201
  99.2 3.2 %copy-start.1 = (bf16[8,2,512,512]{3,2,1,0:T(8,128)(2,1)}, bf16[8,2,512,512]{3,2,1,0:T(8,128)(2,1)S(1)}, u32[]{:S(2)}) copy-start(bf16[8,2,512,512]{3,2,1,0:T(8,128)(2,1)S(1)} %get-tuple-element.8.rows_ref) | copy-start | bytes 25165828
Sparse Core Ops, SparseCore 0:
  17.2 90.7 all-gather.1

commit v5 on v4

--- a/solution.py
+++ b/solution.py
@@ -15,6 +15,7 @@
 BF16 = jnp.bfloat16
 MIB = 1024 * 1024
 PARTS = 8
+STEPS = (192, 288, 384, 512)
 
 
 def pack(gives, place, gate_weight, up_weight, down_weight):
@@ -79,7 +80,10 @@
         packed_ref[target, :] = jnp.zeros((16, 128), F32)
         return carry
 
-    lax.fori_loop(starts[4], jnp.where(starts[4] > 16, 32, 16), clear, 0)
+    limit = jnp.int32(STEPS[-1] // 16)
+    for step in STEPS[-2::-1]:
+        limit = jnp.where(starts[4] <= step // 16, step // 16, limit)
+    lax.fori_loop(starts[4], limit, clear, 0)
 
     infac = jnp.zeros((512, 64), F32)
     for plane in range(16):
@@ -153,9 +157,9 @@
             mat = mats[pair * 64 : pair * 64 + 64]
             pair_ref[pair] = jnp.where(lane < 64, mat[:32], mat[32:]).astype(BF16)
 
-    few = live_blocks(place)[1][4] <= 16
-    pl.when(few)(lambda: run(256))
-    pl.when(jnp.logical_not(few))(lambda: run(512))
+    total = live_blocks(place)[1][4] * 16
+    for below, step in zip((-1,) + STEPS, STEPS):
+        pl.when(jnp.logical_and(total > below, total <= step))(lambda step=step: run(step))
 
 
 def layer(place, rows, weights, infac, scale, out_twice):

time: 142 us -> 140 us (0.986)
  Pallas kernels: 16.9 us -> 14.7 us
    pallas_call x1, Pallas kernels: 7.9 us -> 6.03 us  [layer(): pl.pallas_call(layer_kernel, in_specs=[pl.BlockSpec(memory_space=pltpu.SM...]
  transfers between devices with their start and end apart: 4 -> 4, of which waited for: 3 -> 3; matrix products, arithmetic and copies ran while one was open for 3% -> 3% of each run, Pallas kernels for 6% -> 5%
where the time goes in v5:
time: 140 us
  blocking collectives  75.1 us (54%)
  between operations  16.9 us (12%)
  Pallas kernels  14.7 us (10%)
  starting transfers between devices  13.7 us (10%)
  waiting for transfers between devices  10.1 us (7%)
  local copies, waits for them, and re-layouts  7.2 us (5%)
  other arithmetic  1.57 us (1%)
    all_to_all x1, blocking collectives, per_device(): lax.all_to_all(jnp.broadcast_to(acts[None], (16, 512, 256)), PLANE, 0, 0)  56.8 us
    all_to_all x1, blocking collectives, per_device(): parts = lax.all_to_all(spread, ('xh',) + TEST, 0, 0)  18.2 us
    pallas_call x1, Pallas kernels, order(): pl.pallas_call(order_kernel, in_specs=[pl.BlockSpec(memory_space=pltpu.SM...  6.43 us
    pallas_call x1, Pallas kernels, layer(): pl.pallas_call(layer_kernel, in_specs=[pl.BlockSpec(memory_space=pltpu.SM...  6.03 us
    all_gather x1, waiting for transfers between devices, per_device(): weights = lax.all_gather(block, 'z').reshape(4096, 768)  5.98 us
    ppermute x1, starting transfers between devices, per_device(): other = lax.ppermute(own, 'c', swap)  5.49 us
    ppermute x1, starting transfers between devices, per_device(): lax.ppermute(pack(True, place, gate_weight, up_weight, down_weight), 'xh'...  5.48 us
    unnamed x17, local copies, waits for them, and re-layouts  4.7 us
  transfers between devices with their start and end apart: 4, of which 3 were waited for; matrix products, arithmetic and copies ran while one was open for 3% of the time, Pallas kernels for 5%

profile of v5, /device:TPU:1, one launch (start us, length us, event | category | flops | bytes accessed | tf_op | source)
XLA Modules:
  0.0 140.1 jit_solution(3958624757011380331)
XLA Ops:
  6.5 0.0 copy-start
  6.5 0.0 all-gather.2.cloned.1.call-start
  6.5 0.1 pad_add_fusion.1.place
  6.6 1.2 shard_map.100
  7.8 5.5 %collective-permute-start.1 = (bf16[128,768]{1,0:T(8,128)(2,1)S(1)}, bf16[128,768]{1,0:T(8,128)(2,1)S(1)}, u32[]{:S(2)}, u32[]{:S(2)}) collective-permute-start(bf16[128,768]{1,0:T(8,128)(2,1)S(1)} %shard_map.100), channel_id=1, source_target_pairs={{0,256},{256,0},{1,257},{257,1},{2,258},{258,2},{3,259},{259,3},{4... | collective-permute-start | bytes 589832 | tf_op jit(solution)/shard_map/ppermute | solution.py:194
  13.3 1.1 shard_map.102
  14.4 1.9 %collective-permute-done.1 = bf16[128,768]{1,0:T(8,128)(2,1)S(1)} collective-permute-done((bf16[128,768]{1,0:T(8,128)(2,1)S(1)}, bf16[128,768]{1,0:T(8,128)(2,1)S(1)}, u32[]{:S(2)}, u32[]{:S(2)}) %collective-permute-start.1) | collective-permute-done | bytes 196640 | tf_op jit(solution)/shard_map/ppermute | solution.py:194
  16.3 0.0 copy-start.2
  16.3 0.8 copy-done.2
  17.1 0.0 all-gather.2.cloned.1.call-update
  17.1 0.5 slice.37
  18.3 1.0 maximum_add_fusion
  19.3 0.4 broadcast_in_dim.17
  19.7 0.0 copy-start.5
  19.7 0.0 copy-start.6
  19.8 0.0 copy-start.4
  19.8 0.0 copy-start.3
  19.8 56.8 %all_to_all.10 = bf16[16,512,256]{2,1,0:T(8,128)(2,1)} all-to-all(bf16[16,512,256]{2,1,0:T(8,128)(2,1)S(1)} %broadcast_in_dim.17), channel_id=1, replica_groups=mesh['xh'=2,'z'=16,'y'=4,'xl'=2,'c'=2] {'xh','y','xl'}, dimensions={0} | all-to-all | bytes 8388608 | tf_op jit(solution)/shard_map/all_to_all | solution.py:200
  76.6 5.5 %collective-permute-start.2 = (bf16[2,2,4,512,256]{4,3,2,1,0:T(8,128)(2,1)}, bf16[2,2,4,512,256]{4,3,2,1,0:T(8,128)(2,1)}, u32[]{:S(2)}, u32[]{:S(2)}) collective-permute-start(bf16[2,2,4,512,256]{4,3,2,1,0:T(8,128)(2,1)} %bitcast.8.own_ref), channel_id=1, source_target_pairs={{0,1},{1,0},{2,3},{3,2},{4,5},{5,4},{6,7},{7,6},{8,9},{9,8},{10,11... | collective-permute-start | bytes 12582920 | tf_op jit(solution)/shard_map/ppermute | solution.py:201
  82.1 0.0 copy-done.5
  82.1 0.6 fusion.3
  84.0 0.0 copy-done.6
  84.0 0.6 fusion.4
  85.9 0.1 fusion
  86.0 2.7 %collective-permute-start = (f32[1,128]{1,0:T(1,128)S(1)}, f32[1,128]{1,0:T(1,128)S(1)}, u32[]{:S(2)}, u32[]{:S(2)}) collective-permute-start(f32[1,128]{1,0:T(1,128)S(1)} %fusion), channel_id=1, source_target_pairs={{0,256},{256,0},{1,257},{257,1},{2,258},{258,2},{3,259},{259,3},{4... | collective-permute-start | bytes 1544 | tf_op jit(solution)/shard_map/ppermute | solution.py:205
  88.7 0.0 copy-done.4
  88.7 0.1 copy.23
  88.9 0.1 copy.24
  89.0 0.1 pad_maximum_fusion.out_ref
  89.1 0.0 copy-done.3
  89.1 0.5 copy.20.in_ref
  89.6 2.2 %collective-permute-done = f32[1,128]{1,0:T(1,128)S(1)} collective-permute-done((f32[1,128]{1,0:T(1,128)S(1)}, f32[1,128]{1,0:T(1,128)S(1)}, u32[]{:S(2)}, u32[]{:S(2)}) %collective-permute-start) | collective-permute-done | bytes 544 | tf_op jit(solution)/shard_map/ppermute | solution.py:205
  91.8 0.1 fusion.2
  91.9 0.1 convert_element_type.26
  92.0 0.1 pad_add_fusion.place
  92.1 0.1 slice_reduce_fusion
  92.2 0.1 compare_select_fusion
  92.3 0.0 collective-permute-done.2.other_ref
  92.3 0.1 broadcast_in_dim.35.scale_ref
  92.4 6.4 %shard_map.101 = (bf16[8,2,512,512]{3,2,1,0:T(8,128)(2,1)S(1)}, f32[512,128]{1,0:T(8,128)S(1)}, f32[512,128]{1,0:T(8,128)S(1)}) custom-call(s32[7]{0:T(128)S(1)} %pad_add_fusion.place, bf16[2,2,4,512,256]{4,3,2,1,0:T(8,128)(2,1)} %bitcast.8.own_ref, bf16[2,2,4,512,256]{4,3,2,1,0:T(8,128)(2,1)} %collective-permute-done.2.other_ref, ...), custom_call_target="tpu_custom_call" | custom-call | flops 268435456 | bytes 17825792 | tf_op jit(solution)/shard_map/pallas_call | solution.py:106
  98.9 0.0 copy-start.1
  98.9 3.2 %copy-done.1 = bf16[8,2,512,512]{3,2,1,0:T(8,128)(2,1)} copy-done((bf16[8,2,512,512]{3,2,1,0:T(8,128)(2,1)}, bf16[8,2,512,512]{3,2,1,0:T(8,128)(2,1)S(1)}, u32[]{:S(2)}) %copy-start.1) | copy-done | bytes 8388632
  102.1 6.0 %all-gather.2.cloned.1.call-done = bf16[16,2,128,768]{3,2,1,0:T(8,128)(2,1)} async-done(((bf16[1,2,128,768]{3,2,1,0:T(8,128)(2,1)}), bf16[16,2,128,768]{3,2,1,0:T(8,128)(2,1)}) %all-gather.2.cloned.1.call-update) | async-done | bytes 6291472 | tf_op jit(solution)/shard_map/all_gather | solution.py:197
  108.0 6.0 %shard_map.103 = bf16[2,32,128]{2,1,0:T(8,128)(2,1)S(1)} custom-call(s32[7]{0:T(128)S(1)} %pad_add_fusion.place, bf16[8,2,512,512]{3,2,1,0:T(8,128)(2,1)} %copy-done.1, bf16[4096,768]{1,0:T(8,128)(2,1)} %bitcast.21, f32[512,128]{1,0:T(8,128)S(1)} %get-tuple-element.9.infac_ref, f32[512,128]{1,0:T(8,128)S(1)} %get-tuple-element.10.scale_ref, ...), custom_call_target="tpu_custom_call" | custom-call | flops 3221225472 | bytes 15728640 | tf_op jit(solution)/shard_map/pallas_call | solution.py:170
  114.1 18.2 %all_to_all.11 = bf16[32,32,128]{2,1,0:T(8,128)(2,1)S(1)} all-to-all(bf16[32,32,128]{2,1,0:T(8,128)(2,1)S(1)} %bitcast.22), channel_id=1, replica_groups=mesh['xh'=2,'z'=16,'y'=4,'xl'=2,'c'=2] {'xh','y','xl','c'}, dimensions={0} | all-to-all | bytes 524288 | tf_op jit(solution)/shard_map/all_to_all | solution.py:220
  132.4 0.1 reduce_sum.12
  132.4 0.0 copy-done
  132.4 0.8 fusion.5
  (8 shorter events, 0.1 us)
Async XLA Ops:
  6.5 125.9 %copy-start = (bf16[64,4096]{1,0:T(8,128)(2,1)S(1)}, bf16[64,4096]{1,0:T(8,128)(2,1)}, u32[]{:S(2)}) copy-start(bf16[64,4096]{1,0:T(8,128)(2,1)} %param.19) | copy-start | bytes 1572868
  6.5 101.5 %all-gather.2.cloned.1.call-start = ((), (), s32[]{:S(2)}) async-start(), calls=%async_computation.2 | async-start | bytes 6684672 | tf_op jit(solution)/shard_map/all_gather | solution.py:197
  7.8 8.5 %collective-permute-start.1 = (bf16[128,768]{1,0:T(8,128)(2,1)S(1)}, bf16[128,768]{1,0:T(8,128)(2,1)S(1)}, u32[]{:S(2)}, u32[]{:S(2)}) collective-permute-start(bf16[128,768]{1,0:T(8,128)(2,1)S(1)} %shard_map.100), channel_id=1, source_target_pairs={{0,256},{256,0},{1,257},{257,1},{2,258},{258,2},{3,259},{259,3},{4... | collective-permute-start | bytes 589832 | tf_op jit(solution)/shard_map/ppermute | solution.py:194
  16.3 0.8 copy-start.2
  19.7 62.4 %copy-start.5 = (f32[1,2]{1,0:T(1,128)S(1)}, f32[1,2]{1,0:T(1,128)}, u32[]{:S(2)}) copy-start(f32[1,2]{1,0:T(1,128)} %param.12) | copy-start | bytes 28
  19.7 64.2 %copy-start.6 = (s32[1,2]{1,0:T(1,128)S(1)}, s32[1,2]{1,0:T(1,128)}, u32[]{:S(2)}) copy-start(s32[1,2]{1,0:T(1,128)} %param.13) | copy-start | bytes 28
  19.8 69.0 %copy-start.4 = (bf16[512,64]{0,1:T(8,128)(2,1)S(1)}, bf16[512,64]{0,1:T(8,128)(2,1)}, u32[]{:S(2)}) copy-start(bf16[512,64]{0,1:T(8,128)(2,1)} %param.18) | copy-start | bytes 196612
  19.8 69.4 %copy-start.3 = (bf16[4096,64]{0,1:T(8,128)(2,1)S(1)}, bf16[4096,64]{0,1:T(8,128)(2,1)}, u32[]{:S(2)}) copy-start(bf16[4096,64]{0,1:T(8,128)(2,1)} %param.17) | copy-start | bytes 1572868
  76.6 15.7 %collective-permute-start.2 = (bf16[2,2,4,512,256]{4,3,2,1,0:T(8,128)(2,1)}, bf16[2,2,4,512,256]{4,3,2,1,0:T(8,128)(2,1)}, u32[]{:S(2)}, u32[]{:S(2)}) collective-permute-start(bf16[2,2,4,512,256]{4,3,2,1,0:T(8,128)(2,1)} %bitcast.8.own_ref), channel_id=1, source_target_pairs={{0,1},{1,0},{2,3},{3,2},{4,5},{5,4},{6,7},{7,6},{8,9},{9,8},{10,11... | collective-permute-start | bytes 12582920 | tf_op jit(solution)/shard_map/ppermute | solution.py:201
  86.0 5.9 %collective-permute-start = (f32[1,128]{1,0:T(1,128)S(1)}, f32[1,128]{1,0:T(1,128)S(1)}, u32[]{:S(2)}, u32[]{:S(2)}) collective-permute-start(f32[1,128]{1,0:T(1,128)S(1)} %fusion), channel_id=1, source_target_pairs={{0,256},{256,0},{1,257},{257,1},{2,258},{258,2},{3,259},{259,3},{4... | collective-permute-start | bytes 1544 | tf_op jit(solution)/shard_map/ppermute | solution.py:205
  98.9 3.2 %copy-start.1 = (bf16[8,2,512,512]{3,2,1,0:T(8,128)(2,1)}, bf16[8,2,512,512]{3,2,1,0:T(8,128)(2,1)S(1)}, u32[]{:S(2)}) copy-start(bf16[8,2,512,512]{3,2,1,0:T(8,128)(2,1)S(1)} %get-tuple-element.8.rows_ref) | copy-start | bytes 25165828
Sparse Core Ops, SparseCore 0:
  17.2 90.7 all-gather.1
